TPU v7x, 32 devices: a whole 2x2x4 slice. The times are simulated.
32 devices in a mesh: dp: 8 (over z, y), blk: 4 (over x, core).
Axes of the slice: x: 2, y: 2, z: 4, core: 2. Of those that a mesh axis runs over, the one named last changes fastest.
Arguments:
- tokens: bfloat16 [8, 1024, 768], P('dp', 'blk'), may hold values from -6 to 6
- lengths: int32 [8, 5], P('dp'), may hold values from 40 to 197, as said below
- w_qkv: bfloat16 [768, 2304], replicated, may hold values from -0.3125 to 0.3125
- w_out: bfloat16 [768, 768], replicated, may hold values from -0.4375 to 0.4375
- w_up: bfloat16 [768, 3072], replicated, may hold values from -0.21875 to 0.21875
- w_down: bfloat16 [3072, 768], replicated, may hold values from -0.15625 to 0.15625
- vectors: float32 [10752], replicated, may hold values from -0.3 to 2.5
- cotangent: bfloat16 [8, 1024, 768], P('dp', 'blk'), may hold values from -6 to 6
Outputs:
- out: bfloat16 [8, 1024, 768], P('dp', 'blk')
- grad_tokens: bfloat16 [8, 1024, 768], P('dp', 'blk')
- grad_w_qkv: float32 [768, 2304], P('blk', 'dp')
- grad_w_out: float32 [768, 768], P('blk', 'dp')
- grad_w_up: float32 [768, 3072], P('blk', 'dp')
- grad_w_down: float32 [3072, 768], P('blk', 'dp')
- grad_vectors: float32 [10752], P(('dp', 'blk'))
Inputs may be any that keep to these rules, and one draw needn't show every extreme that they name: `lengths`: images fill a set's packing places in order from place 0 and padding fills the rest; in every set one image has exactly 197 visible patches and each other image 40 to 197.
All inputs are finite; a program needn't handle non-finite values.
Results may differ from a plain program's by a relative error of at most 0.022.
Values may be sent and summed in bfloat16 or wider, within the bound.
No kernel may reach another device: no remote copies, remote signals or barrier semaphores. Data moves between devices by JAX's collectives and lax.ppermute only.
A program may use at most 128 MiB of HBM per device.

v0:
```python
import math

import jax
import jax.numpy as jnp
from jax import lax
from jax.sharding import PartitionSpec as P

H = 12


EPSILON = 1e-06
FLOOR_SCORE = -1e30


def passed_along(array, axis, by):
    length = lax.axis_size(axis)
    return lax.ppermute(array, axis, [(i, (i + by) % length) for i in range(length)])


def norm_rows(values, gain, shift):
    centre = jnp.mean(values, axis=-1, keepdims=True)
    centred = values - centre
    spread = jnp.mean(centred * centred, axis=-1, keepdims=True)
    return centred * lax.rsqrt(spread + EPSILON) * gain + shift


def exact_gelu(values):
    return jax.nn.gelu(values, approximate=False)


def segment_of(rows_index, rows, parts, ends):
    place = rows_index % rows * parts + rows_index // rows
    return jnp.sum((place[:, None] >= ends[None, :]).astype(jnp.int32), axis=1)


def contract_rows(left, right):
    return lax.dot_general(
        left, right, (((0,), (0,)), ((), ())), preferred_element_type=jnp.float32
    )


def contract_cols(left, right):
    return lax.dot_general(
        left, right, (((1,), (1,)), ((), ())), preferred_element_type=jnp.float32
    )


def attend_block(query, query_item, keys, values, key_item, scale, carry):
    best, total, weighted = carry
    count = keys.shape[0]
    heads = query.shape[1]
    key_heads = keys.reshape(count, heads, -1)
    value_heads = values.reshape(count, heads, -1)
    allowed = (query_item[:, None] == key_item[None, :])[None]
    score = jnp.einsum("qhd,khd->hqk", query, key_heads, preferred_element_type=jnp.float32) * scale
    score = jnp.where(allowed, score, FLOOR_SCORE)
    newbest = jnp.maximum(best, jnp.max(score, axis=-1))
    weight = jnp.where(allowed, jnp.exp(score - newbest[..., None]), 0.0)
    factor = jnp.exp(best - newbest)
    total = total * factor + jnp.sum(weight, axis=-1)
    weighted = weighted * factor[..., None] + jnp.einsum(
        "hqk,khd->hqd", weight.astype(jnp.bfloat16), value_heads, preferred_element_type=jnp.float32
    )
    return (newbest, total, weighted)


def grad_block(query, d_out, logsum, delta, query_item, keys, values, key_item, scale):
    count = keys.shape[0]
    heads = query.shape[1]
    key_heads = keys.reshape(count, heads, -1)
    value_heads = values.reshape(count, heads, -1)
    allowed = (query_item[:, None] == key_item[None, :])[None]
    score = jnp.einsum("qhd,khd->hqk", query, key_heads, preferred_element_type=jnp.float32) * scale
    prob = jnp.where(allowed, jnp.exp(score - logsum[..., None]), 0.0)
    d_prob = jnp.einsum("qhd,khd->hqk", d_out, value_heads, preferred_element_type=jnp.float32)
    d_score = (prob * (d_prob - delta[..., None])).astype(jnp.bfloat16)
    d_query = (
        jnp.einsum("hqk,khd->qhd", d_score, key_heads, preferred_element_type=jnp.float32) * scale
    )
    d_keys = jnp.einsum("hqk,qhd->khd", d_score, query, preferred_element_type=jnp.float32) * scale
    d_values = jnp.einsum(
        "hqk,qhd->khd", prob.astype(jnp.bfloat16), d_out, preferred_element_type=jnp.float32
    )
    return (d_query, d_keys.reshape(count, -1), d_values.reshape(count, -1))


def on_device(tokens, lengths, w_qkv, w_out, w_up, w_down, vectors, cotangent):
    inputs = tokens[0].astype(jnp.float32)
    rows, width = inputs.shape
    heads = H
    head_size = width // heads
    scale = head_size ** (-0.5)
    items = lengths.shape[1]
    ends = jnp.cumsum(lengths[0])
    parts = lax.axis_size("blk")
    position = lax.axis_index("blk")
    query_item = segment_of(position * rows + lax.iota(jnp.int32, rows), rows, parts, ends)
    valid = (query_item < items).astype(jnp.float32)[:, None]
    pieces = [vectors[index * width : (index + 1) * width] for index in range(10)]
    (
        gain_one,
        shift_one,
        bias_q,
        bias_v,
        bias_o,
        scale_one,
        gain_two,
        shift_two,
        bias_d,
        scale_two,
    ) = pieces
    bias_up = vectors[10 * width :]
    normed, norm_one_pull = jax.vjp(norm_rows, inputs, gain_one, shift_one)
    normed_low = normed.astype(jnp.bfloat16)
    qkv_bias = jnp.concatenate([bias_q, jnp.zeros_like(bias_q), bias_v])
    projected = (jnp.dot(normed_low, w_qkv, preferred_element_type=jnp.float32) + qkv_bias).astype(
        jnp.bfloat16
    )
    query = projected[:, :width].reshape(rows, heads, head_size)
    keys = projected[:, width : 2 * width]
    values = projected[:, 2 * width :]
    start_state = (
        jnp.full((heads, rows), FLOOR_SCORE, jnp.float32),
        jnp.zeros((heads, rows), jnp.float32),
        jnp.zeros((heads, rows, head_size), jnp.float32),
    )
    carry = start_state
    piece = (
        lax.all_gather(keys, "blk", axis=0, tiled=True),
        lax.all_gather(values, "blk", axis=0, tiled=True),
    )
    count = piece[0].shape[0]
    size = math.gcd(count, 512)
    steps = count // size
    key_blocks = piece[0].reshape(steps, size, width)
    value_blocks = piece[1].reshape(steps, size, width)

    def inner(state, item):
        block_keys, block_values, offset = item
        key_item = segment_of(offset + lax.iota(jnp.int32, size), rows, parts, ends)
        return (
            attend_block(query, query_item, block_keys, block_values, key_item, scale, state),
            None,
        )

    carry, unused = lax.scan(
        inner, carry, (key_blocks, value_blocks, lax.iota(jnp.int32, steps) * size)
    )
    best, total, weighted = carry
    logsum = best + jnp.log(total)
    attended = (weighted / total[..., None]).transpose(1, 0, 2).reshape(rows, width)
    attended_low = attended.astype(jnp.bfloat16)
    branch = jnp.dot(attended_low, w_out, preferred_element_type=jnp.float32) + bias_o
    mid = inputs + scale_one * branch
    normed_two, norm_two_pull = jax.vjp(norm_rows, mid, gain_two, shift_two)
    normed_two_low = normed_two.astype(jnp.bfloat16)
    before = jnp.dot(normed_two_low, w_up, preferred_element_type=jnp.float32) + bias_up
    activated, gelu_pull = jax.vjp(exact_gelu, before)
    activated_low = activated.astype(jnp.bfloat16)
    feed = jnp.dot(activated_low, w_down, preferred_element_type=jnp.float32) + bias_d
    result = mid + scale_two * feed
    out = (result * valid).astype(jnp.bfloat16)
    d_result = cotangent[0].astype(jnp.float32) * valid
    d_feed = (scale_two * d_result).astype(jnp.bfloat16)
    g_scale_two = jnp.sum(d_result * feed, axis=0)
    g_bias_d = jnp.sum(d_feed.astype(jnp.float32), axis=0)
    g_w_down = contract_rows(activated_low, d_feed)
    d_activated = contract_cols(d_feed, w_down)
    d_before = gelu_pull(d_activated)[0].astype(jnp.bfloat16)
    g_bias_up = jnp.sum(d_before.astype(jnp.float32), axis=0)
    g_w_up = contract_rows(normed_two_low, d_before)
    d_normed_two = contract_cols(d_before, w_up)
    d_mid_norm, g_gain_two, g_shift_two = norm_two_pull(d_normed_two)
    d_mid = d_result + d_mid_norm
    d_branch = (scale_one * d_mid).astype(jnp.bfloat16)
    g_scale_one = jnp.sum(d_mid * branch, axis=0)
    g_bias_o = jnp.sum(d_branch.astype(jnp.float32), axis=0)
    g_w_out = contract_rows(attended_low, d_branch)
    d_attended = contract_cols(d_branch, w_out).astype(jnp.bfloat16)
    d_heads = d_attended.reshape(rows, heads, head_size)
    delta = jnp.sum(
        (d_attended.astype(jnp.float32) * attended).reshape(rows, heads, head_size), axis=-1
    ).T
    zero_query = jnp.zeros((rows, heads, head_size), jnp.float32)

    def visit_block(block_keys, block_values, owner):
        key_item = segment_of(owner * rows + lax.iota(jnp.int32, rows), rows, parts, ends)
        return grad_block(
            query, d_heads, logsum, delta, query_item, block_keys, block_values, key_item, scale
        )

    def send_back(d_keys, d_values):
        return (
            passed_along(d_keys.astype(jnp.bfloat16), "blk", 1).astype(d_keys.dtype),
            passed_along(d_values.astype(jnp.bfloat16), "blk", 1).astype(d_values.dtype),
        )

    def accumulate(state, owner):
        d_query, block_keys, block_values, d_keys, d_values = state
        dq_part, dk_part, dv_part = visit_block(block_keys, block_values, owner)
        d_keys, d_values = send_back(d_keys + dk_part, d_values + dv_part)
        return (d_query + dq_part, d_keys, d_values)

    def turn(step, state):
        owner = (position - step) % parts
        d_query, d_keys, d_values = accumulate(state, owner)
        block_keys, block_values = passed_along((state[1], state[2]), "blk", 1)
        return (d_query, block_keys, block_values, d_keys, d_values)

    zero_rows = jnp.zeros((rows, width), jnp.float32)
    state = lax.fori_loop(0, parts - 1, turn, (zero_query, keys, values, zero_rows, zero_rows))
    d_query, d_keys, d_values = accumulate(state, (position + 1) % parts)
    d_projected = jnp.concatenate([d_query.reshape(rows, width), d_keys, d_values], axis=1).astype(
        jnp.bfloat16
    )
    g_bias_q = jnp.sum(d_projected[:, :width].astype(jnp.float32), axis=0)
    g_bias_v = jnp.sum(d_projected[:, 2 * width :].astype(jnp.float32), axis=0)
    g_w_qkv = contract_rows(normed_low, d_projected)
    d_normed = contract_cols(d_projected, w_qkv)
    d_input_norm, g_gain_one, g_shift_one = norm_one_pull(d_normed)
    d_inputs = d_mid + d_input_norm
    g_vectors = jnp.concatenate(
        [
            g_gain_one,
            g_shift_one,
            g_bias_q,
            g_bias_v,
            g_bias_o,
            g_scale_one,
            g_gain_two,
            g_shift_two,
            g_bias_d,
            g_scale_two,
            g_bias_up,
        ]
    )
    column_sums = (
        lax.psum_scatter(
            g_w_qkv.astype(jnp.bfloat16), "dp", scatter_dimension=1, tiled=True
        ).astype(jnp.float32),
        lax.psum_scatter(
            g_w_out.astype(jnp.bfloat16), "dp", scatter_dimension=1, tiled=True
        ).astype(jnp.float32),
        lax.psum_scatter(g_w_up.astype(jnp.bfloat16), "dp", scatter_dimension=1, tiled=True).astype(
            jnp.float32
        ),
        lax.psum_scatter(
            g_w_down.astype(jnp.bfloat16), "dp", scatter_dimension=1, tiled=True
        ).astype(jnp.float32),
        lax.psum_scatter(
            g_vectors.astype(jnp.bfloat16), "dp", scatter_dimension=0, tiled=True
        ).astype(jnp.float32),
    )
    g_w_qkv, g_w_out, g_w_up, g_w_down, g_vectors = (
        lax.psum_scatter(
            column_sums[0].astype(jnp.bfloat16), "blk", scatter_dimension=0, tiled=True
        ).astype(jnp.float32),
        lax.psum_scatter(
            column_sums[1].astype(jnp.bfloat16), "blk", scatter_dimension=0, tiled=True
        ).astype(jnp.float32),
        lax.psum_scatter(
            column_sums[2].astype(jnp.bfloat16), "blk", scatter_dimension=0, tiled=True
        ).astype(jnp.float32),
        lax.psum_scatter(
            column_sums[3].astype(jnp.bfloat16), "blk", scatter_dimension=0, tiled=True
        ).astype(jnp.float32),
        lax.psum_scatter(
            column_sums[4].astype(jnp.bfloat16), "blk", scatter_dimension=0, tiled=True
        ).astype(jnp.float32),
    )
    return (
        out[None],
        d_inputs.astype(jnp.bfloat16)[None],
        g_w_qkv,
        g_w_out,
        g_w_up,
        g_w_down,
        g_vectors,
    )


def solution(mesh):
    return jax.shard_map(
        on_device,
        mesh=mesh,
        in_specs=(
            P("dp", "blk", None),
            P("dp", None),
            P(),
            P(),
            P(),
            P(),
            P(),
            P("dp", "blk", None),
        ),
        out_specs=(
            P("dp", "blk", None),
            P("dp", "blk", None),
            P("blk", "dp"),
            P("blk", "dp"),
            P("blk", "dp"),
            P("blk", "dp"),
            P(("dp", "blk")),
        ),
        check_vma=False,
    )
```

profile of v0, /device:TPU:0, one launch (start us, length us, event | category | flops | bytes accessed | tf_op | source)
XLA Modules:
  0.0 648.6 jit_solution(878322957962141117)
XLA Ops:
  28.2 9.4 %all-gather.3.cloned.1.call-done = bf16[1024,768]{1,0:T(8,128)(2,1)} async-done(((bf16[256,768]{1,0:T(8,128)(2,1)}), bf16[1024,768]{1,0:T(8,128)(2,1)}) %all-gather.3.cloned.1.call-update) | async-done | bytes 1572880 | tf_op jit(solution)/shard_map/all_gather | solution.py:129
  37.6 21.8 %all-gather.5.cloned.1.call-done = bf16[1024,768]{1,0:T(8,128)(2,1)} async-done(((bf16[256,768]{1,0:T(8,128)(2,1)}), bf16[1024,768]{1,0:T(8,128)(2,1)}) %all-gather.5.cloned.1.call-update) | async-done | bytes 1572880 | tf_op jit(solution)/shard_map/all_gather | solution.py:130
  59.4 59.2 %while.42 = (s32[]{:T(128)}, f32[12,256]{1,0:T(8,128)}, f32[12,256]{1,0:T(8,128)}, f32[12,256,64]{1,2,0:T(8,128)}, s32[256]{0:T(256)}, /*index=5*/s32[2]{0:T(128...) while((s32[]{:T(128)}, f32[12,256]{1,0:T(8,128)}, ...), condition=%wide.region_8.9_spmd.clone, body=%wide.region_4.8_spmd.clone.sunk | while | flops 423855104 | bytes 29582596 | solution.py:146
  63.5 2.7 constant_dynamic-slice_fusion.3
  66.2 2.3 copy.74
  68.5 5.7 fusion.170
  74.9 4.3 fusion.171
  81.0 2.3 copy.75
  83.3 5.5 fusion.173
  93.0 2.7 constant_dynamic-slice_fusion.3
  95.7 2.3 copy.74
  98.0 5.7 fusion.170
  104.4 4.3 fusion.171
  110.5 2.3 copy.75
  112.8 5.8 fusion.173
  120.8 2.3 copy.57
  123.1 3.2 fusion.97
  126.6 10.9 %multiply_convert_fusion.2 = (bf16[256,3072]{1,0:T(8,128)(2,1)}, f32[256,3072]{1,0:T(8,128)S(1)}, f32[256,3072]{1,0:T(8,128)S(1)}) fusion(f32[3072]{0:T(1024)S(1)} %copy-done.42, bf16[768,3072]{1,0:T(8,128)(2,1)} %param.16, f32[256,768]{1,0:T(8,128)S(1)} %get-tuple-element.762, f32[768]{0:T(1024)S(1)} %copy-done.26, f32[768]{0:T(1024)S(1)} %copy-done.25, ...), kind=kOutput, calls=%fused_computation.69 | convolution fusion | flops 1260847104 | bytes 13389824 | tf_op jit(solution)/shard_map/dot_general | solution.py:157
  137.6 2.8 fusion.102
  147.1 3.1 convert_multiply_fusion.1
  152.1 2.3 copy.58
  156.3 93.1 %while.43 = (s32[]{:T(128)}, f32[256,12,64]{0,2,1:T(8,128)}, bf16[256,768]{0,1:T(8,128)(2,1)}, bf16[256,768]{0,1:T(8,128)(2,1)}, f32[256,768]{0,1:T(8,128)}, /*i...) while((s32[]{:T(128)}, f32[256,12,64]{0,2,1:T(8,128)}, ...), condition=%wide.region_16.17_spmd.clone, body=%wide.region_14.16_spmd.clone.sunk | while | flops 513614848 | bytes 50276012 | solution.py:211
  163.3 2.6 multiply_convert_fusion.7
  171.1 3.0 fusion.186
  183.2 4.2 collective-permute-done.1
  194.3 2.6 multiply_convert_fusion.7
  202.1 3.2 fusion.186
  211.9 2.3 collective-permute-done
  214.2 4.2 collective-permute-done.1
  225.3 2.6 multiply_convert_fusion.7
  233.1 3.2 fusion.186
  242.9 2.3 collective-permute-done
  245.2 4.2 collective-permute-done.1
  252.6 2.6 multiply_convert_fusion.1
  256.5 2.3 fusion.101
  259.7 4.2 collective-permute-done.4
  264.7 3.0 convolution_convert_fusion
  268.4 5.4 convolution_convert_fusion.2
  273.8 6.8 %copy.68 = bf16[768,3072]{0,1:T(8,128)(2,1)} copy(bf16[768,3072]{1,0:T(8,128)(2,1)} %convolution_convert_fusion.2) | data formatting | bytes 9437184
  281.2 5.1 convolution_convert_fusion.1
  288.3 58.8 %reduce-scatter.15.cloned.1.call-done = bf16[768,288]{0,1:T(8,128)(2,1)} async-done(((bf16[768,2304]{0,1:T(8,128)(2,1)}), bf16[768,288]{0,1:T(8,128)(2,1)}) %reduce-scatter.15.cloned.1.call-update) | async-done | bytes 442384 | tf_op jit(solution)/shard_map/reduce_scatter | solution.py:238
  349.2 96.2 %reduce-scatter.29.cloned.1.call-done = bf16[384,768]{1,0:T(8,128)(2,1)} async-done(((bf16[3072,768]{1,0:T(8,128)(2,1)}), bf16[384,768]{1,0:T(8,128)(2,1)}) %reduce-scatter.29.cloned.1.call-update) | async-done | bytes 589840
  452.1 4.0 fusion.93
  456.6 87.4 %reduce-scatter.21.cloned.1.call-done = bf16[3072,96]{0,1:T(8,128)(2,1)} async-done(((bf16[3072,768]{0,1:T(8,128)(2,1)}), bf16[3072,96]{0,1:T(8,128)(2,1)}) %reduce-scatter.21.cloned.1.call-update) | async-done | bytes 589840 | tf_op jit(solution)/shard_map/reduce_scatter | solution.py:247
  555.8 6.9 %fusion.68 = (bf16[768]{0:T(1024)(128)(2,1)}, bf16[768]{0:T(1024)(128)(2,1)}, bf16[1,256,768]{2,1,0:T(8,128)(2,1)}, bf16[1,256,768]{2,1,0:T(8,128)(2,1)}) fusion(bf16[1,256,768]{2,1,0:T(8,128)(2,1)} %param.19, f32[256]{0:T(256)S(1)} %copy-done.48, f32[256,768]{1,0:T(8,128)} %get-tuple-element.783, f32[256,768]{1,0:T(8,128)} %copy-done.13, ...), kind=kOutput, calls=%fused_computation.125 | convolution fusion | flops 1212480000 | bytes 11028480 | tf_op jit(solution)/shard_map/dot_general | solution.py:160
  571.3 37.2 %all-reduce = bf16[10752]{0:T(1024)(128)(2,1)} all-reduce(bf16[10752]{0:T(1024)(128)(2,1)} %dynamic-update-slice.10), channel_id=10, replica_groups=mesh['dp'=8,'blk'=4] {'dp'}, use_global_device_ids=true, to_apply=%region_39.40.clone | all-reduce | flops 10752 | bytes 43008
  609.3 6.1 all-reduce.1
  624.3 15.9 %reduce-scatter.23.cloned.1.call-done = bf16[768,96]{0,1:T(8,128)(2,1)} async-done(((bf16[3072,96]{0,1:T(8,128)(2,1)}), bf16[768,96]{0,1:T(8,128)(2,1)}) %reduce-scatter.23.cloned.1.call-update) | async-done | bytes 147472 | tf_op jit(solution)/shard_map/reduce_scatter | solution.py:264
  (329 shorter events, 154.1 us)
Async XLA Ops:
  7.2 30.4 %all-gather.3.cloned.1.call-start = ((), (), s32[]{:S(2)}) async-start(), calls=%async_computation.8 | async-start | bytes 1966080 | tf_op jit(solution)/shard_map/all_gather | solution.py:129
  8.8 5.1 copy-start.54
  14.0 7.1 %copy-start.57 = (s32[1,5]{1,0:T(1,128)S(1)}, s32[1,5]{1,0:T(1,128)}, u32[]{:S(2)}) copy-start(s32[1,5]{1,0:T(1,128)} %param.13) | copy-start | bytes 64
  15.1 44.3 %all-gather.5.cloned.1.call-start = ((), (), s32[]{:S(2)}) async-start(), calls=%async_computation.9 | async-start | bytes 1966080 | tf_op jit(solution)/shard_map/all_gather | solution.py:130
  15.8 270.6 %reduce-scatter.17.cloned.1.call-start = ((), (), s32[]{:S(2)}) async-start(), calls=%async_computation.11 | async-start | bytes 1327104 | tf_op jit(solution)/shard_map/reduce_scatter | solution.py:241
  120.8 5.8 copy-start.25
  120.8 5.8 copy-start.26
  123.1 14.5 %slice-start.2 = ((s8[4718592]{0:T(1024)(128)(4,1)}), s8[4194304]{0:T(1024)(128)(4,1)S(1)}, s32[]{:S(2)}) async-start(s8[4718592]{0:T(1024)(128)(4,1)} %bitcast.231), calls=%async_computation.20 | async-start | bytes 8388608
  123.1 17.3 %slice-start = ((s8[4718592]{0:T(1024)(128)(4,1)}), s8[4194304]{0:T(1024)(128)(4,1)S(1)}, s32[]{:S(2)}) async-start(s8[4718592]{0:T(1024)(128)(4,1)} %bitcast.229), calls=%async_computation.18 | async-start | bytes 8388608
  126.3 16.3 %copy-start.9 = (f32[256,768]{1,0:T(8,128)}, f32[256,768]{1,0:T(8,128)S(1)}, u32[]{:S(2)}) copy-start(f32[256,768]{1,0:T(8,128)S(1)} %get-tuple-element.762) | copy-start | bytes 2359300
  126.3 16.3 %copy-start.30 = (f32[256]{0:T(256)}, f32[256]{0:T(256)S(1)}, u32[]{:S(2)}) copy-start(f32[256]{0:T(256)S(1)} %broadcast_multiply_fusion) | copy-start | bytes 3076
  126.5 16.1 %copy-start.41 = (f32[256]{0:T(256)}, f32[256]{0:T(256)S(1)}, u32[]{:S(2)}) copy-start(f32[256]{0:T(256)S(1)} %fusion.79) | copy-start | bytes 3076
  126.6 11.0 %copy-start.16 = (bf16[1,256,768]{2,1,0:T(8,128)(2,1)S(1)}, bf16[1,256,768]{2,1,0:T(8,128)(2,1)}, u32[]{:S(2)}) copy-start(bf16[1,256,768]{2,1,0:T(8,128)(2,1)} %param.19) | copy-start | bytes 1179652
  126.6 11.0 %copy-start.28 = (f32[768]{0:T(1024)S(1)}, f32[768]{0:T(1024)}, u32[]{:S(2)}) copy-start(f32[768]{0:T(1024)} %get-tuple-element.773) | copy-start | bytes 9220
  126.6 11.0 %copy-start.46 = (f32[256]{0:T(256)S(1)}, f32[256]{0:T(256)}, u32[]{:S(2)}) copy-start(f32[256]{0:T(256)} %compare_convert_fusion) | copy-start | bytes 3076
  126.6 11.0 %slice-start.3 = ((s8[4718592]{0:T(1024)(128)(4,1)}), s8[524288]{0:T(1024)(128)(4,1)S(1)}, s32[]{:S(2)}) async-start(s8[4718592]{0:T(1024)(128)(4,1)} %bitcast.231), calls=%async_computation.21 | async-start | bytes 1048576
  126.6 13.8 %slice-start.1 = ((s8[4718592]{0:T(1024)(128)(4,1)}), s8[524288]{0:T(1024)(128)(4,1)S(1)}, s32[]{:S(2)}) async-start(s8[4718592]{0:T(1024)(128)(4,1)} %bitcast.229), calls=%async_computation.19 | async-start | bytes 1048576
  156.3 190.8 %reduce-scatter.15.cloned.1.call-start = ((), (), s32[]{:S(2)}) async-start(), calls=%async_computation.10 | async-start | bytes 3981312 | tf_op jit(solution)/shard_map/reduce_scatter | solution.py:238
  167.2 7.5 %collective-permute-start.2 = (bf16[256,768]{0,1:T(8,128)(2,1)}, bf16[256,768]{0,1:T(8,128)(2,1)}, u32[]{:S(2)}, u32[]{:S(2)}) collective-permute-start(bf16[256,768]{0,1:T(8,128)(2,1)} %fusion.187), channel_id=1, source_target_pairs={{0,1},{1,2},{2,3},{3,0},{4,5},{5,6},{6,7},{7,4},{8,9},{9,10},{10,1... | collective-permute-start | bytes 1179656 | tf_op jit(solution)/shard_map/while/body/eval_jaxpr/ppermute | solution.py:17
  169.1 9.9 %collective-permute-start.3 = (bf16[256,768]{0,1:T(8,128)(2,1)}, bf16[256,768]{0,1:T(8,128)(2,1)}, u32[]{:S(2)}, u32[]{:S(2)}) collective-permute-start(bf16[256,768]{0,1:T(8,128)(2,1)} %fusion.189), channel_id=1, source_target_pairs={{0,1},{1,2},{2,3},{3,0},{4,5},{5,6},{6,7},{7,4},{8,9},{9,10},{10,1... | collective-permute-start | bytes 1179656 | tf_op jit(solution)/shard_map/while/body/eval_jaxpr/ppermute | solution.py:17
  169.3 13.9 %collective-permute-start = (bf16[256,768]{0,1:T(8,128)(2,1)}, bf16[256,768]{0,1:T(8,128)(2,1)}, u32[]{:S(2)}, u32[]{:S(2)}) collective-permute-start(bf16[256,768]{0,1:T(8,128)(2,1)} %copy.96), channel_id=1, source_target_pairs={{0,1},{1,2},{2,3},{3,0},{4,5},{5,6},{6,7},{7,4},{8,9},{9,10},{10,1... | collective-permute-start | bytes 1179656 | tf_op jit(solution)/shard_map/while/body/eval_jaxpr/ppermute | solution.py:17
  169.5 17.9 %collective-permute-start.1 = (bf16[256,768]{0,1:T(8,128)(2,1)}, bf16[256,768]{0,1:T(8,128)(2,1)}, u32[]{:S(2)}, u32[]{:S(2)}) collective-permute-start(bf16[256,768]{0,1:T(8,128)(2,1)} %copy.97), channel_id=1, source_target_pairs={{0,1},{1,2},{2,3},{3,0},{4,5},{5,6},{6,7},{7,4},{8,9},{9,10},{10,1... | collective-permute-start | bytes 1179656 | tf_op jit(solution)/shard_map/while/body/eval_jaxpr/ppermute | solution.py:17
  198.2 7.5 %collective-permute-start.2 = (bf16[256,768]{0,1:T(8,128)(2,1)}, bf16[256,768]{0,1:T(8,128)(2,1)}, u32[]{:S(2)}, u32[]{:S(2)}) collective-permute-start(bf16[256,768]{0,1:T(8,128)(2,1)} %fusion.187), channel_id=1, source_target_pairs={{0,1},{1,2},{2,3},{3,0},{4,5},{5,6},{6,7},{7,4},{8,9},{9,10},{10,1... | collective-permute-start | bytes 1179656 | tf_op jit(solution)/shard_map/while/body/eval_jaxpr/ppermute | solution.py:17
  199.9 10.1 %collective-permute-start.3 = (bf16[256,768]{0,1:T(8,128)(2,1)}, bf16[256,768]{0,1:T(8,128)(2,1)}, u32[]{:S(2)}, u32[]{:S(2)}) collective-permute-start(bf16[256,768]{0,1:T(8,128)(2,1)} %fusion.189), channel_id=1, source_target_pairs={{0,1},{1,2},{2,3},{3,0},{4,5},{5,6},{6,7},{7,4},{8,9},{9,10},{10,1... | collective-permute-start | bytes 1179656 | tf_op jit(solution)/shard_map/while/body/eval_jaxpr/ppermute | solution.py:17
  200.3 13.8 %collective-permute-start = (bf16[256,768]{0,1:T(8,128)(2,1)}, bf16[256,768]{0,1:T(8,128)(2,1)}, u32[]{:S(2)}, u32[]{:S(2)}) collective-permute-start(bf16[256,768]{0,1:T(8,128)(2,1)} %copy.96), channel_id=1, source_target_pairs={{0,1},{1,2},{2,3},{3,0},{4,5},{5,6},{6,7},{7,4},{8,9},{9,10},{10,1... | collective-permute-start | bytes 1179656 | tf_op jit(solution)/shard_map/while/body/eval_jaxpr/ppermute | solution.py:17
  200.3 18.1 %collective-permute-start.1 = (bf16[256,768]{0,1:T(8,128)(2,1)}, bf16[256,768]{0,1:T(8,128)(2,1)}, u32[]{:S(2)}, u32[]{:S(2)}) collective-permute-start(bf16[256,768]{0,1:T(8,128)(2,1)} %copy.97), channel_id=1, source_target_pairs={{0,1},{1,2},{2,3},{3,0},{4,5},{5,6},{6,7},{7,4},{8,9},{9,10},{10,1... | collective-permute-start | bytes 1179656 | tf_op jit(solution)/shard_map/while/body/eval_jaxpr/ppermute | solution.py:17
  229.2 7.5 %collective-permute-start.2 = (bf16[256,768]{0,1:T(8,128)(2,1)}, bf16[256,768]{0,1:T(8,128)(2,1)}, u32[]{:S(2)}, u32[]{:S(2)}) collective-permute-start(bf16[256,768]{0,1:T(8,128)(2,1)} %fusion.187), channel_id=1, source_target_pairs={{0,1},{1,2},{2,3},{3,0},{4,5},{5,6},{6,7},{7,4},{8,9},{9,10},{10,1... | collective-permute-start | bytes 1179656 | tf_op jit(solution)/shard_map/while/body/eval_jaxpr/ppermute | solution.py:17
  230.9 10.1 %collective-permute-start.3 = (bf16[256,768]{0,1:T(8,128)(2,1)}, bf16[256,768]{0,1:T(8,128)(2,1)}, u32[]{:S(2)}, u32[]{:S(2)}) collective-permute-start(bf16[256,768]{0,1:T(8,128)(2,1)} %fusion.189), channel_id=1, source_target_pairs={{0,1},{1,2},{2,3},{3,0},{4,5},{5,6},{6,7},{7,4},{8,9},{9,10},{10,1... | collective-permute-start | bytes 1179656 | tf_op jit(solution)/shard_map/while/body/eval_jaxpr/ppermute | solution.py:17
  231.3 13.8 %collective-permute-start = (bf16[256,768]{0,1:T(8,128)(2,1)}, bf16[256,768]{0,1:T(8,128)(2,1)}, u32[]{:S(2)}, u32[]{:S(2)}) collective-permute-start(bf16[256,768]{0,1:T(8,128)(2,1)} %copy.96), channel_id=1, source_target_pairs={{0,1},{1,2},{2,3},{3,0},{4,5},{5,6},{6,7},{7,4},{8,9},{9,10},{10,1... | collective-permute-start | bytes 1179656 | tf_op jit(solution)/shard_map/while/body/eval_jaxpr/ppermute | solution.py:17
  231.3 18.0 %collective-permute-start.1 = (bf16[256,768]{0,1:T(8,128)(2,1)}, bf16[256,768]{0,1:T(8,128)(2,1)}, u32[]{:S(2)}, u32[]{:S(2)}) collective-permute-start(bf16[256,768]{0,1:T(8,128)(2,1)} %copy.97), channel_id=1, source_target_pairs={{0,1},{1,2},{2,3},{3,0},{4,5},{5,6},{6,7},{7,4},{8,9},{9,10},{10,1... | collective-permute-start | bytes 1179656 | tf_op jit(solution)/shard_map/while/body/eval_jaxpr/ppermute | solution.py:17
  252.5 7.3 %collective-permute-start.5 = (bf16[256,768]{0,1:T(8,128)(2,1)S(1)}, bf16[256,768]{0,1:T(8,128)(2,1)S(1)}, u32[]{:S(2)}, u32[]{:S(2)}) collective-permute-start(bf16[256,768]{0,1:T(8,128)(2,1)S(1)} %fusion.62), channel_id=1, source_target_pairs={{0,1},{1,2},{2,3},{3,0},{4,5},{5,6},{6,7},{7,4},{8,9},{9,10},{10,1... | collective-permute-start | bytes 1179656 | tf_op jit(solution)/shard_map/ppermute | solution.py:17
  255.6 9.1 %copy-start.11 = (bf16[1,256,768]{2,1,0:T(8,128)(2,1)S(1)}, bf16[1,256,768]{2,1,0:T(8,128)(2,1)}, u32[]{:S(2)}) copy-start(bf16[1,256,768]{2,1,0:T(8,128)(2,1)} %param.12) | copy-start | bytes 1179652
  255.6 9.1 %copy-start.33 = (f32[768]{0:T(1024)S(1)}, f32[768]{0:T(1024)}, u32[]{:S(2)}) copy-start(f32[768]{0:T(1024)} %copy-done.32) | copy-start | bytes 9220
  255.6 9.1 %copy-start.44 = (f32[256]{0:T(256)S(1)}, f32[256]{0:T(256)}, u32[]{:S(2)}) copy-start(f32[256]{0:T(256)} %copy-done.43) | copy-start | bytes 3076
  255.6 9.1 %copy-start.52 = (f32[256]{0:T(256)S(1)}, f32[256]{0:T(256)}, u32[]{:S(2)}) copy-start(f32[256]{0:T(256)} %copy-done.51) | copy-start | bytes 3076
  255.6 9.1 %copy-start.55 = (f32[768]{0:T(1024)S(1)}, f32[768]{0:T(1024)}, u32[]{:S(2)}) copy-start(f32[768]{0:T(1024)} %copy-done.54) | copy-start | bytes 9220
  255.8 8.1 %collective-permute-start.4 = (bf16[256,768]{0,1:T(8,128)(2,1)S(1)}, bf16[256,768]{0,1:T(8,128)(2,1)S(1)}, u32[]{:S(2)}, u32[]{:S(2)}) collective-permute-start(bf16[256,768]{0,1:T(8,128)(2,1)S(1)} %fusion.63), channel_id=1, source_target_pairs={{0,1},{1,2},{2,3},{3,0},{4,5},{5,6},{6,7},{7,4},{8,9},{9,10},{10,1... | collective-permute-start | bytes 1179656 | tf_op jit(solution)/shard_map/ppermute | solution.py:17
  258.8 5.1 copy-start.21
  267.8 177.6 %reduce-scatter.29.cloned.1.call-start = ((), (), s32[]{:S(2)}) async-start(), calls=%async_computation.17 | async-start | bytes 5308416
  280.6 263.3 %reduce-scatter.21.cloned.1.call-start = ((), (), s32[]{:S(2)}) async-start(), calls=%async_computation.13 | async-start | bytes 5308416 | tf_op jit(solution)/shard_map/reduce_scatter | solution.py:247
  286.4 165.1 %copy-start.35 = (bf16[12,64]{1,0:T(8,128)(2,1)S(1)}, bf16[12,64]{1,0:T(8,128)(2,1)}, u32[]{:S(2)}) copy-start(bf16[12,64]{1,0:T(8,128)(2,1)} %get-tuple-element.789) | copy-start | bytes 4612
  286.4 165.7 %copy-start.34 = (f32[768]{0:T(1024)S(1)}, f32[768]{0:T(1024)}, u32[]{:S(2)}) copy-start(f32[768]{0:T(1024)} %copy-done.32) | copy-start | bytes 9220
  286.4 165.7 %copy-start.45 = (f32[256]{0:T(256)S(1)}, f32[256]{0:T(256)}, u32[]{:S(2)}) copy-start(f32[256]{0:T(256)} %copy-done.43) | copy-start | bytes 3076
  286.4 329.7 %reduce-scatter.27.cloned.1.call-start = ((), (), s32[]{:S(2)}) async-start(), calls=%async_computation.16 | async-start | bytes 245760
  288.2 330.9 %reduce-scatter.25.cloned.1.call-start = ((), (), s32[]{:S(2)}) async-start(), calls=%async_computation.15 | async-start | bytes 737280
  349.2 273.4 %reduce-scatter.19.cloned.1.call-start = ((), (), s32[]{:S(2)}) async-start(), calls=%async_computation.12 | async-start | bytes 737280 | tf_op jit(solution)/shard_map/reduce_scatter | solution.py:261
  447.6 192.6 %reduce-scatter.23.cloned.1.call-start = ((), (), s32[]{:S(2)}) async-start(), calls=%async_computation.14 | async-start | bytes 737280 | tf_op jit(solution)/shard_map/reduce_scatter | solution.py:264
  452.1 103.7 %copy-start.48 = (f32[256]{0:T(256)S(1)}, f32[256]{0:T(256)}, u32[]{:S(2)}) copy-start(f32[256]{0:T(256)} %compare_convert_fusion) | copy-start | bytes 3076
  (55 other events, 145.7 us)
Sparse Core Ops, SparseCore 0:
  15.2 22.3 all-gather.2
  39.7 19.6 all-gather.4
  156.4 64.0 reduce-scatter.16
  267.9 79.1 reduce-scatter.14
  350.6 94.7 reduce-scatter.28
  448.9 95.0 reduce-scatter.20
  547.0 19.5 reduce-scatter.26
  569.0 22.0 reduce-scatter.24
  593.6 22.1 reduce-scatter.18
  618.1 21.9 reduce-scatter.22
where the time goes:
time: 652 us; the launch traced here: 649 us
  waiting for transfers between devices  323 us (50%)
  matrix products  107 us (16%)
  local copies, waits for them, and re-layouts  89 us (14%)
  other arithmetic  61.7 us (9%)
  blocking collectives  43.3 us (7%)
  between operations  16.1 us (2%)
  starting transfers between devices  7.92 us (1%)
    unnamed x13, waiting for transfers between devices  97 us
    reduce_scatter x1, waiting for transfers between devices, on_device(): lax.psum_scatter(g_w_down.astype(jnp.bfloat16), 'dp', scatter_dimension=1...  87.4 us
    reduce_scatter x1, waiting for transfers between devices, on_device(): lax.psum_scatter(g_w_qkv.astype(jnp.bfloat16), 'dp', scatter_dimension=1,...  58.8 us
    unnamed x127, local copies, waits for them, and re-layouts  44.5 us
    unnamed x2, blocking collectives  43.3 us
    ppermute x14, waiting for transfers between devices, passed_along(): lax.ppermute(array, axis, [(i, (i + by) % length) for i in range(length)])  32.9 us
    all_gather x1, waiting for transfers between devices, on_device(): lax.all_gather(values, 'blk', axis=0, tiled=True)  21.8 us
    dynamic_slice x8, local copies, waits for them, and re-layouts, on_device(): lax.scan(inner, carry, (key_blocks, value_blocks, lax.iota(jnp.int32, ste...  17 us
  transfers between devices with their start and end apart: 24, of which 20 were waited for; matrix products, arithmetic and copies ran while one was open for 23% of the time, Pallas kernels for 0%

commit v1 on v0

--- a/solution.py
+++ b/solution.py
@@ -1,11 +1,16 @@
+import functools
 import math
 
 import jax
 import jax.numpy as jnp
 from jax import lax
+from jax.experimental import pallas as pl
+from jax.experimental.pallas import tpu as pltpu
 from jax.sharding import PartitionSpec as P
 
 H = 12
+HEAD_SIZE = 64
+TILE = 64
 
 
 EPSILON = 1e-06
@@ -279,28 +284,820 @@
     )
 
 
+BF = jnp.bfloat16
+F32 = jnp.float32
+MASKED = -1e30
+VMEM_BYTES = 48 * 1024 * 1024
+
+
+def dot_nn(left, right):
+    return lax.dot_general(left, right, (((1,), (0,)), ((), ())), preferred_element_type=F32)
+
+
+def dot_nt(left, right):
+    return lax.dot_general(left, right, (((1,), (1,)), ((), ())), preferred_element_type=F32)
+
+
+def dot_tn(left, right):
+    return lax.dot_general(left, right, (((0,), (0,)), ((), ())), preferred_element_type=F32)
+
+
+def standardise(values):
+    centred = values - jnp.mean(values, axis=-1, keepdims=True)
+    inverse = lax.rsqrt(jnp.mean(centred * centred, axis=-1, keepdims=True) + EPSILON)
+    return centred * inverse, inverse
+
+
+def standardise_grad(grad, xhat, inverse):
+    first = jnp.mean(grad, axis=-1, keepdims=True)
+    second = jnp.mean(grad * xhat, axis=-1, keepdims=True)
+    return (grad - first - xhat * second) * inverse
+
+
+def column_sum(values):
+    return jnp.sum(values, axis=0, keepdims=True)
+
+
+def item_at(place, where_ref, items):
+    found = jnp.zeros_like(place)
+    for index in range(items):
+        found = found + (place >= where_ref[4 + index]).astype(jnp.int32)
+    return found
+
+
+def own_block(where_ref, rel_x, rel_c):
+    return 2 * (where_ref[0] ^ rel_x) + (where_ref[1] ^ rel_c)
+
+
+def valid_rows(where_ref, rel_c, rows, parts, items):
+    row = lax.broadcasted_iota(jnp.int32, (rows, 1), 0)
+    item = item_at(row * parts + own_block(where_ref, 0, rel_c), where_ref, items)
+    return (item < items).astype(F32)
+
+
+def chip_call(body, grid, in_specs, out_specs, out_shape, scratch=(), flops=0, moved=0):
+    return pl.pallas_call(
+        body,
+        grid_spec=pltpu.PrefetchScalarGridSpec(
+            num_scalar_prefetch=1,
+            grid=grid,
+            in_specs=in_specs,
+            out_specs=out_specs,
+            scratch_shapes=list(scratch),
+        ),
+        out_shape=out_shape,
+        compiler_params=pltpu.CompilerParams(
+            vmem_limit_bytes=VMEM_BYTES, dimension_semantics=("arbitrary",) * len(grid)
+        ),
+        cost_estimate=pl.CostEstimate(flops=flops, bytes_accessed=moved, transcendentals=0),
+    )
+
+
+def whole(*shape):
+    return pl.BlockSpec(shape, lambda *at: (0,) * len(shape))
+
+
+def shaped(shape, dtype):
+    return jax.ShapeDtypeStruct(shape, dtype)
+
+
+def local_qkv_kernel(
+    where_ref, own_ref, sib_ref, vec_ref, bias_ref, weight_ref, normed_ref, query_ref, key_ref, value_ref
+):
+    rows = own_ref.shape[0]
+    for rel_c, ref in enumerate((own_ref, sib_ref)):
+        xhat, unused = standardise(ref[...].astype(F32))
+        normed_ref[rel_c * rows : (rel_c + 1) * rows] = (xhat * vec_ref[0:1] + vec_ref[1:2]).astype(BF)
+    projected = dot_nn(normed_ref[...], weight_ref[...])
+    half = projected.shape[1] // 3
+    scale = HEAD_SIZE ** (-0.5)
+    query = ((projected[:, :half] + bias_ref[0:1]).astype(BF).astype(F32) * scale).astype(BF)
+    key_ref[...] = projected[:, half : 2 * half].astype(BF)
+    value_ref[...] = (projected[:, 2 * half :] + bias_ref[1:2]).astype(BF)
+    for tile in range(rows // TILE):
+        for rel_c in range(2):
+            query_ref[(2 * tile + rel_c) * TILE : (2 * tile + rel_c + 1) * TILE] = query[
+                rel_c * rows + tile * TILE : rel_c * rows + (tile + 1) * TILE
+            ]
+
+
+def feed_grad_kernel(parts, items, where_ref, own_ref, sib_ref, vec_ref, down_ref, dact_ref, turned_ref, sum_ref, held):
+    rows = own_ref.shape[0]
+
+    @pl.when(pl.program_id(0) == 0)
+    def first():
+        for rel_c, ref in enumerate((own_ref, sib_ref)):
+            valid = valid_rows(where_ref, rel_c, rows, parts, items)
+            part = (vec_ref[9:10] * (ref[...].astype(F32) * valid)).astype(BF)
+            held[rel_c * rows : (rel_c + 1) * rows] = part
+        turned_ref[...] = held[...].T
+        sum_ref[...] = column_sum(held[:rows].astype(F32))
+
+    dact_ref[...] = dot_nt(held[...], down_ref[...]).astype(BF)
+
+
+def lanes_below(shape, count):
+    return lax.broadcasted_iota(jnp.int32, shape, 1) < count
+
+
+def stack_heads(pair):
+    low = lanes_below(pair.shape, HEAD_SIZE)
+    zero = jnp.zeros_like(pair)
+    return jnp.concatenate([jnp.where(low, pair, zero), jnp.where(low, zero, pair)], axis=0)
+
+
+def join_heads(stacked_turned):
+    stacked = stacked_turned.T
+    count = stacked.shape[0] // 2
+    return jnp.where(
+        lanes_below((count, stacked.shape[1]), HEAD_SIZE), stacked[:count], stacked[count:]
+    )
+
+
+def query_items(where_ref, tile, parts, items):
+    lane = lax.broadcasted_iota(jnp.int32, (1, 4 * TILE), 1)
+    rel_c = (lane // TILE) % 2
+    block = 2 * where_ref[0] + (where_ref[1] ^ rel_c)
+    return item_at((tile * TILE + lane % TILE) * parts + block, where_ref, items)
+
+
+def key_items(where_ref, first, count, parts, items):
+    row = lax.broadcasted_iota(jnp.int32, (count * parts * TILE, 1), 0)
+    tile = first + row // (parts * TILE)
+    slot = (row // TILE) % parts
+    block = 2 * (where_ref[0] ^ (slot // 2)) + (where_ref[1] ^ (slot % 2))
+    return item_at((tile * TILE + row % TILE) * parts + block, where_ref, items)
+
+
+def item_of_place(where_ref, place, items):
+    found = jnp.int32(0)
+    for index in range(items):
+        found = found + (place >= where_ref[4 + index]).astype(jnp.int32)
+    return found
+
+
+def tiles_meet(where_ref, one, other, parts, items):
+    span = TILE * parts
+    low, high = min(one, other), max(one, other)
+    return item_of_place(where_ref, low * span + span - 1, items) >= item_of_place(
+        where_ref, high * span, items
+    )
+
+
+def near_tiles(tile, tiles):
+    return max(0, tile - 1), min(tiles, tile + 2)
+
+
+def attend_kernel(
+    parts, items, where_ref, far_a_ref, far_b_ref, vec_ref, bias_ref, weight_ref, query_ref, key_ref, value_ref,
+    normed_ref, keys_ref, values_ref, attended_ref, logsum_ref, best_ref, total_ref, mixed_ref,
+):
+    rows = far_a_ref.shape[0]
+    tiles = rows // TILE
+    span = parts * TILE
+    width = query_ref.shape[1]
+    for rel_c, ref in enumerate((far_a_ref, far_b_ref)):
+        xhat, unused = standardise(ref[...].astype(F32))
+        normed_ref[rel_c * rows : (rel_c + 1) * rows] = (xhat * vec_ref[0:1] + vec_ref[1:2]).astype(BF)
+    projected = dot_nn(normed_ref[...], weight_ref[:, width:])
+    far_keys = projected[:, :width].astype(BF)
+    far_values = (projected[:, width:] + bias_ref[1:2]).astype(BF)
+    for tile in range(tiles):
+        for slot in range(2):
+            to = slice(tile * span + slot * TILE, tile * span + (slot + 1) * TILE)
+            at = slice(slot * rows + tile * TILE, slot * rows + (tile + 1) * TILE)
+            keys_ref[to] = key_ref[at]
+            values_ref[to] = value_ref[at]
+            to = slice(tile * span + (slot + 2) * TILE, tile * span + (slot + 3) * TILE)
+            keys_ref[to] = far_keys[at]
+            values_ref[to] = far_values[at]
+
+    def pair(index, carry):
+        lanes = pl.ds(pl.multiple_of(index * 2 * HEAD_SIZE, 2 * HEAD_SIZE), 2 * HEAD_SIZE)
+        for tile in range(tiles):
+            query = stack_heads(query_ref[2 * TILE * tile : 2 * TILE * (tile + 1), lanes])
+            query_item = query_items(where_ref, tile, parts, items)
+
+            def visit(first, last):
+                key_item = key_items(where_ref, first, last - first, parts, items)
+                score = dot_nt(keys_ref[first * span : last * span, lanes], query)
+                return jnp.where(key_item == query_item, score, MASKED)
+
+            def mix(weight, first, last):
+                return dot_tn(values_ref[first * span : last * span, lanes], weight.astype(BF))
+
+            first, last = near_tiles(tile, tiles)
+            score = visit(first, last)
+            best = jnp.max(score, axis=0, keepdims=True)
+            weight = jnp.exp(score - best)
+            best_ref[...] = best
+            total_ref[...] = column_sum(weight)
+            mixed_ref[...] = mix(weight, first, last)
+            for other in range(tiles):
+                if first <= other < last:
+                    continue
+
+                @pl.when(tiles_meet(where_ref, tile, other, parts, items))
+                def far(other=other):
+                    score = visit(other, other + 1)
+                    best = jnp.maximum(best_ref[...], jnp.max(score, axis=0, keepdims=True))
+                    factor = jnp.exp(best_ref[...] - best)
+                    weight = jnp.exp(score - best)
+                    total_ref[...] = total_ref[...] * factor + column_sum(weight)
+                    mixed_ref[...] = mixed_ref[...] * factor + mix(weight, other, other + 1)
+                    best_ref[...] = best
+
+            total = total_ref[...]
+            logsum_ref[pl.ds(index * tiles + tile, 1)] = best_ref[...] + jnp.log(total)
+            attended = join_heads(mixed_ref[...] / total).astype(BF)
+            for rel_c in range(2):
+                attended_ref[rel_c * rows + tile * TILE : rel_c * rows + (tile + 1) * TILE, lanes] = attended[
+                    rel_c * TILE : (rel_c + 1) * TILE
+                ]
+        return carry
+
+    lax.fori_loop(0, width // (2 * HEAD_SIZE), pair, 0)
+
+
+def forward_kernel(
+    parts, items, where_ref, att_own_ref, att_sib_ref, own_ref, sib_ref, vec_ref, bias_ref, out_own_ref, out_sib_ref,
+    up_ref, dact_ref, turned_ref,
+    act_ref, dbefore_ref, down_ref, mid_ref, branch_ref, normed_ref, bias_sum_ref,
+):
+    rows = own_ref.shape[0]
+
+    @pl.when(pl.program_id(0) == 0)
+    def first():
+        for rel_c, ref in enumerate((own_ref, sib_ref)):
+            here = slice(rel_c * rows, (rel_c + 1) * rows)
+            there = slice((1 - rel_c) * rows, (2 - rel_c) * rows)
+            branch = (
+                dot_nn(att_own_ref[here], out_own_ref[...])
+                + dot_nn(att_sib_ref[there], out_sib_ref[...])
+                + vec_ref[4:5]
+            )
+            if rel_c == 0:
+                branch_ref[...] = branch
+            mid = ref[...].astype(F32) + vec_ref[5:6] * branch
+            mid_ref[here] = mid
+            xhat, unused = standardise(mid)
+            normed_ref[here] = (xhat * vec_ref[6:7] + vec_ref[7:8]).astype(BF)
+
+    before = dot_nn(normed_ref[...], up_ref[...]) + bias_ref[...]
+    normal = 0.5 + 0.5 * lax.erf(before * (0.5**0.5))
+    act = (before * normal).astype(BF)
+    act_ref[...] = act
+    slope = normal + before * (jnp.exp(-0.5 * before * before) * ((2.0 * math.pi) ** -0.5))
+    dbefore = (dact_ref[...].astype(F32) * slope).astype(BF)
+    dbefore_ref[...] = dbefore
+    bias_sum_ref[...] = column_sum(dbefore.astype(F32))
+    down_ref[0] = dot_nn(turned_ref[...], act).astype(BF)
+
+
+def up_grad_kernel(rows_block, where_ref, normed_ref, dbefore_ref, keep_ref, send_ref, turned):
+    @pl.when(pl.program_id(0) == 0)
+    def first():
+        turned[...] = normed_ref[...].T
+
+    dbefore = dbefore_ref[...]
+    core = where_ref[1]
+    for at_x in range(2):
+        for ref, block in ((keep_ref, 2 * at_x + core), (send_ref, 2 * at_x + 1 - core)):
+            left = turned[pl.ds(pl.multiple_of(block * rows_block, rows_block), rows_block)]
+            ref[at_x, 0, 0] = dot_nn(left, dbefore).astype(BF)
+
+
+def back_up_kernel(where_ref, dbefore_ref, up_ref, keep_ref, send_ref, total):
+    step = pl.program_id(0)
+
+    @pl.when(step == 0)
+    def first():
+        total[...] = jnp.zeros_like(total)
+
+    total[...] += dot_nt(dbefore_ref[...], up_ref[...])
+
+    @pl.when(step == pl.num_programs(0) - 1)
+    def last():
+        keep_ref[...] = total[...]
+        send_ref[...] = total[...].astype(BF)
+
+
+def feed_kernel(where_ref, act_ref, down_ref, keep_ref, send_ref, total):
+    step = pl.program_id(0)
+    rows = keep_ref.shape[0]
+
+    @pl.when(step == 0)
+    def first():
+        total[...] = jnp.zeros_like(total)
+
+    total[...] += dot_nn(act_ref[...], down_ref[...])
+
+    @pl.when(step == pl.num_programs(0) - 1)
+    def last():
+        keep_ref[...] = total[:rows]
+        send_ref[...] = total[rows:].astype(BF)
+
+
+def result_kernel(parts, items, where_ref, keep_ref, got_ref, mid_ref, cot_ref, vec_ref, out_ref, sum_ref):
+    rows = keep_ref.shape[0]
+    valid = valid_rows(where_ref, 0, rows, parts, items)
+    feed = keep_ref[...] + got_ref[...].astype(F32) + vec_ref[8:9]
+    out_ref[...] = (valid * (mid_ref[...] + vec_ref[9:10] * feed)).astype(BF)
+    sum_ref[...] = column_sum(cot_ref[...].astype(F32) * valid * feed)
+
+
+def middle_kernel(
+    parts, items, where_ref, keep_ref, got_ref, mid_ref, own_ref, sib_ref, vec_ref, att_ref, out_ref, branch_ref,
+    dmid_ref, datt_ref, gout_ref, sum_ref, held,
+):
+    rows = own_ref.shape[0]
+    for rel_c, ref in enumerate((own_ref, sib_ref)):
+        here = slice(rel_c * rows, (rel_c + 1) * rows)
+        there = slice((1 - rel_c) * rows, (2 - rel_c) * rows)
+        valid = valid_rows(where_ref, rel_c, rows, parts, items)
+        dnormed = keep_ref[here] + got_ref[there].astype(F32)
+        xhat, inverse = standardise(mid_ref[here])
+        dmid = ref[...].astype(F32) * valid + standardise_grad(vec_ref[6:7] * dnormed, xhat, inverse)
+        dbranch = (vec_ref[5:6] * dmid).astype(BF)
+        held[here] = dbranch
+        if rel_c == 0:
+            dmid_ref[...] = dmid
+            sum_ref[0:1] = column_sum(dbranch.astype(F32))
+            sum_ref[1:2] = column_sum(dmid * branch_ref[...])
+            sum_ref[2:3] = column_sum(dnormed * xhat)
+            sum_ref[3:4] = column_sum(dnormed)
+    datt_ref[...] = dot_nt(held[...], out_ref[...]).astype(BF)
+    grad = dot_tn(held[...], att_ref[...])
+    count = gout_ref.shape[1]
+    size = grad.shape[0] // count
+    for index in range(count):
+        for side, packed in enumerate(pack_unit(grad[index * size : (index + 1) * size])):
+            gout_ref[side, index] = packed.astype(BF)
+
+
+def pack_unit(unit):
+    half = unit.shape[0] // 2
+    width = unit.shape[1]
+    top, bottom = unit[:half], unit[half:]
+    low = lanes_below((half, width), width // 2)
+    left = jnp.where(low, top, pltpu.roll(bottom, width // 2, 1))
+    right = jnp.where(low, pltpu.roll(top, width // 2, 1), bottom)
+    return left, right
+
+
+def attend_grad_kernel(
+    parts, items, where_ref, query_ref, keys_ref, values_ref, attended_ref, datt_ref, logsum_ref,
+    dquery_ref, dkeys_ref, dvalues_ref, dk, dv, dq,
+):
+    width = query_ref.shape[1]
+    rows = query_ref.shape[0] // 2
+    tiles = rows // TILE
+    span = parts * TILE
+    scale = HEAD_SIZE ** (-0.5)
+
+    def pair(index, carry):
+        lanes = pl.ds(pl.multiple_of(index * 2 * HEAD_SIZE, 2 * HEAD_SIZE), 2 * HEAD_SIZE)
+        dk[...] = jnp.zeros_like(dk)
+        dv[...] = jnp.zeros_like(dv)
+        for tile in range(tiles):
+            query = stack_heads(query_ref[2 * TILE * tile : 2 * TILE * (tile + 1), lanes])
+            query_item = query_items(where_ref, tile, parts, items)
+            places = [slice(rel_c * rows + tile * TILE, rel_c * rows + (tile + 1) * TILE) for rel_c in range(2)]
+            grad = jnp.concatenate([datt_ref[at, lanes] for at in places], axis=0)
+            attended = jnp.concatenate([attended_ref[at, lanes] for at in places], axis=0)
+            product = (grad.astype(F32) * attended.astype(F32)).T
+            delta = jnp.concatenate(
+                [column_sum(product[:HEAD_SIZE]), column_sum(product[HEAD_SIZE:])], axis=1
+            )
+            grad = stack_heads(grad)
+            logsum = logsum_ref[pl.ds(index * tiles + tile, 1)]
+
+            def visit(first, last):
+                at = slice(first * span, last * span)
+                key_item = key_items(where_ref, first, last - first, parts, items)
+                keys = keys_ref[at, lanes]
+                score = dot_nt(keys, query)
+                prob = jnp.exp(jnp.where(key_item == query_item, score, MASKED) - logsum)
+                dprob = dot_nt(values_ref[at, lanes], grad)
+                dscore = (prob * (dprob - delta)).astype(BF)
+                dv[at] += dot_nn(prob.astype(BF), grad)
+                dk[at] += dot_nn(dscore, query)
+                return dot_tn(keys, dscore)
+
+            first, last = near_tiles(tile, tiles)
+            dq[...] = visit(first, last)
+            for other in range(tiles):
+                if first <= other < last:
+                    continue
+
+                @pl.when(tiles_meet(where_ref, tile, other, parts, items))
+                def far(other=other):
+                    dq[...] += visit(other, other + 1)
+
+            dquery = (join_heads(dq[...]) * scale).astype(BF)
+            for rel_c in range(2):
+                dquery_ref[places[rel_c], lanes] = dquery[rel_c * TILE : (rel_c + 1) * TILE]
+        for tile in range(tiles):
+            for slot in range(parts):
+                to = slice(slot * rows + tile * TILE, slot * rows + (tile + 1) * TILE)
+                at = slice(tile * span + slot * TILE, tile * span + (slot + 1) * TILE)
+                dkeys_ref[to, lanes] = dk[at].astype(BF)
+                dvalues_ref[to, lanes] = dv[at].astype(BF)
+        return carry
+
+    lax.fori_loop(0, width // (2 * HEAD_SIZE), pair, 0)
+
+
+def qkv_grad_kernel(where_ref, near_ref, far_ref, dquery_ref, dkeys_ref, dvalues_ref, keep_ref, send_ref, sum_ref):
+    rows = near_ref.shape[0]
+    width = near_ref.shape[1]
+    mine = where_ref[1] == 0
+    sum_ref[0:1] = column_sum(dquery_ref[...].astype(F32))
+    sum_ref[1:2] = column_sum(dvalues_ref[...].astype(F32))
+    for part, ref in enumerate((dquery_ref, dkeys_ref, dvalues_ref)):
+        grad = dot_tn(ref[:rows], near_ref[...])
+        if part:
+            grad = grad + dot_tn(ref[rows:], far_ref[...])
+        size = grad.shape[0] // 4
+        for unit in range(4):
+            for at_x in range(2):
+                left, right = pack_unit(
+                    grad[unit * size : (unit + 1) * size, at_x * width // 2 : (at_x + 1) * width // 2]
+                )
+                keep_ref[at_x, 4 * part + unit] = jnp.where(mine, left, right).astype(BF)
+                send_ref[at_x, 4 * part + unit] = jnp.where(mine, right, left).astype(BF)
+
+
+def tokens_grad_kernel(
+    where_ref, own_ref, sib_ref, far_a_ref, far_b_ref, dquery_ref, dkeys_ref, dvalues_ref, weight_ref,
+    keep_ref, send_ref, sum_ref,
+):
+    rows = own_ref.shape[0]
+    half = dquery_ref.shape[1]
+    gain = jnp.zeros((1, own_ref.shape[1]), F32)
+    shift = gain
+    for slot, ref in enumerate((own_ref, sib_ref, far_a_ref, far_b_ref)):
+        at = slice(slot * rows, (slot + 1) * rows)
+        part = dot_nt(dkeys_ref[at], weight_ref[:, half : 2 * half]) + dot_nt(
+            dvalues_ref[at], weight_ref[:, 2 * half :]
+        )
+        if slot < 2:
+            part = part + dot_nt(dquery_ref[at], weight_ref[:, :half])
+        xhat, unused = standardise(ref[...].astype(F32))
+        gain = gain + column_sum(part * xhat)
+        shift = shift + column_sum(part)
+        if slot % 2:
+            send_ref[slot // 2] = part.astype(BF)
+        else:
+            keep_ref[slot // 2] = part
+    sum_ref[0:1] = gain
+    sum_ref[1:2] = shift
+
+
+def first_norm_grad_kernel(where_ref, keep_ref, got_ref, own_ref, dmid_ref, vec_ref, out_ref):
+    dnormed = keep_ref[...] + got_ref[...].astype(F32)
+    xhat, inverse = standardise(own_ref[...].astype(F32))
+    out_ref[...] = (dmid_ref[...] + standardise_grad(vec_ref[0:1] * dnormed, xhat, inverse)).astype(BF)
+
+
+def to_core(array):
+    length = lax.axis_size("blk")
+    return lax.ppermute(array, "blk", [(i, i ^ 1) for i in range(length)])
+
+
+def to_x(array):
+    length = lax.axis_size("blk")
+    return lax.ppermute(array, "blk", [(i, i ^ 2) for i in range(length)])
+
+
+def to_y(array):
+    length = lax.axis_size("dp")
+    return lax.ppermute(array, "dp", [(i, i ^ 1) for i in range(length)])
+
+
+def along_z(array, by):
+    length = lax.axis_size("dp")
+    return lax.ppermute(array, "dp", [(i, (i + 2 * by) % length) for i in range(length)])
+
+
+def picked(array, index, axis):
+    return lax.dynamic_index_in_dim(array, index, axis, keepdims=False)
+
+
+def added(one, other):
+    return (one.astype(F32) + other.astype(F32)).astype(BF)
+
+
+def sum_to_owner(blocks, at, first_rows):
+    x, z, y = at
+    one, two = blocks[..., :first_rows, :], blocks[..., first_rows:, :]
+    one_got = to_x(picked(one, 1 - x, 0))
+    two_got = to_y(picked(two, 1 - y, 2))
+    one = added(one_got, picked(one, x, 0))
+    two = added(two_got, picked(two, y, 2))
+    one_got = to_y(picked(one, 1 - y, 1))
+    two_got = to_x(picked(two, 1 - x, 0))
+    one = added(one_got, picked(one, y, 1))
+    two = added(two_got, picked(two, x, 0))
+    joined = jnp.concatenate([one, two], axis=1)
+    length = joined.shape[0]
+    got = [along_z(picked(joined, (z + by) % length, 0), by) for by in range(1, length)]
+    total = picked(joined, z, 0).astype(F32)
+    for part in got:
+        total = total + part.astype(F32)
+    return total
+
+
+def unpacked(units):
+    count, half, lanes = units.shape
+    return units.reshape(count, half, 2, lanes // 2).transpose(0, 2, 1, 3).reshape(-1, lanes // 2)
+
+
+def on_device_aligned(tokens, lengths, w_qkv, w_out, w_up, w_down, vectors, cotangent):
+    tokens, cotangent = tokens[0], cotangent[0]
+    rows, width = tokens.shape
+    hidden = w_up.shape[1]
+    items = lengths.shape[1]
+    parts = lax.axis_size("blk")
+    sets = lax.axis_size("dp")
+    position, turn = lax.axis_index("blk"), lax.axis_index("dp")
+    x, core, z, y = position // 2, position % 2, turn // 2, turn % 2
+    where = jnp.concatenate([jnp.stack([x, core, z, y]).astype(jnp.int32), jnp.cumsum(lengths[0]).astype(jnp.int32)])
+    half = width // 2
+    inner = hidden // 2
+    piece = hidden // sets
+    steps = inner // piece
+    both = 2 * rows
+    total_rows = parts * rows
+    block = width // parts
+    names = (parts, items)
+
+    far_a = to_x(tokens)
+    sib = to_core(tokens)
+    cot_sib = to_core(cotangent)
+    far_b = to_core(far_a)
+
+    vec = vectors[: 10 * width].reshape(10, width)
+    bias_up = picked(vectors[10 * width :].reshape(2, 2, -1), core, 1).reshape(1, inner)
+    bias_qv = picked(vec[2:4].reshape(2, 2, 2, block), core, 2).reshape(2, half)
+    w_qkv_own = picked(w_qkv.reshape(width, 3, 2, 2, block), core, 3).reshape(width, 3 * half)
+    w_out_cut = w_out.reshape(2, 2, block, width)
+    w_out_own = picked(w_out_cut, core, 1).reshape(half, width)
+    w_out_sib = picked(w_out_cut, 1 - core, 1).reshape(half, width)
+
+    def unit_of(step, where_ref):
+        return 4 * (step // 2) + 2 * where_ref[1] + step % 2
+
+    up_spec = pl.BlockSpec((width, piece), lambda j, w: (0, unit_of(j, w)))
+    down_spec = pl.BlockSpec((piece, width), lambda j, w: (unit_of(j, w), 0))
+    wide_spec = pl.BlockSpec((both, piece), lambda j, w: (0, j))
+    vec_spec = whole(10, width)
+
+    normed_near, query, key_near, value_near = chip_call(
+        local_qkv_kernel,
+        (1,),
+        [whole(rows, width), whole(rows, width), vec_spec, whole(2, half), whole(width, 3 * half)],
+        [whole(both, width), whole(both, half), whole(both, half), whole(both, half)],
+        [shaped((both, width), BF)] + [shaped((both, half), BF)] * 3,
+        flops=2 * both * width * 3 * half,
+        moved=4 * 2**20,
+    )(where, tokens, sib, vec, bias_qv, w_qkv_own)
+
+    dact, dfeed_turned, bias_d_sum = chip_call(
+        functools.partial(feed_grad_kernel, *names),
+        (steps,),
+        [whole(rows, width), whole(rows, width), vec_spec, down_spec],
+        [wide_spec, whole(width, both), whole(1, width)],
+        [shaped((both, inner), BF), shaped((width, both), BF), shaped((1, width), F32)],
+        scratch=[pltpu.VMEM((both, width), BF)],
+        flops=2 * both * width * inner,
+        moved=5 * 2**20,
+    )(where, cotangent, cot_sib, vec, w_down)
+
+    tiles = rows // TILE
+    pairs = half // (2 * HEAD_SIZE)
+    normed_far, keys, values, attended, logsum = chip_call(
+        functools.partial(attend_kernel, *names),
+        (1,),
+        [whole(rows, width), whole(rows, width), vec_spec, whole(2, half), whole(width, 3 * half)]
+        + [whole(both, half)] * 3,
+        [whole(both, width), whole(total_rows, half), whole(total_rows, half), whole(both, half), whole(pairs * tiles, 4 * TILE)],
+        [shaped((both, width), BF), shaped((total_rows, half), BF), shaped((total_rows, half), BF), shaped((both, half), BF), shaped((pairs * tiles, 4 * TILE), F32)],
+        scratch=[pltpu.VMEM((1, 4 * TILE), F32), pltpu.VMEM((1, 4 * TILE), F32), pltpu.VMEM((2 * HEAD_SIZE, 4 * TILE), F32)],
+        flops=4 * both * width * half + 4 * both * total_rows * half,
+        moved=8 * 2**20,
+    )(where, far_a, far_b, vec, bias_qv, w_qkv_own, query, key_near, value_near)
+
+    attended_sib = to_core(attended)
+
+    act, dbefore, gdown, mid, branch, normed_two, bias_up_sum = chip_call(
+        functools.partial(forward_kernel, *names),
+        (steps,),
+        [whole(both, half), whole(both, half), whole(rows, width), whole(rows, width), vec_spec,
+         pl.BlockSpec((1, piece), lambda j, w: (0, j)), whole(half, width), whole(half, width), up_spec, wide_spec,
+         whole(width, both)],
+        [wide_spec, wide_spec, pl.BlockSpec((1, width, piece), lambda j, w: (j // 2, 0, j % 2)),
+         whole(both, width), whole(rows, width), whole(both, width), pl.BlockSpec((1, piece), lambda j, w: (0, j))],
+        [shaped((both, inner), BF), shaped((both, inner), BF), shaped((2, width, inner // 2), BF),
+         shaped((both, width), F32), shaped((rows, width), F32), shaped((both, width), BF), shaped((1, inner), F32)],
+        flops=2 * both * width * (width + 2 * inner),
+        moved=12 * 2**20,
+    )(where, attended, attended_sib, tokens, sib, vec, bias_up, w_out_own, w_out_sib, w_up, dact, dfeed_turned)
+
+    at = (x, z, y)
+    zs = sets // 2
+    down_blocks = gdown.reshape(2, zs, 2, width // sets, inner // 2)
+    down_total = sum_to_owner(down_blocks, at, width // sets // 2)
+    g_w_down = down_total.T
+
+    swap_spec = pl.BlockSpec((2, 1, 1, block, piece), lambda j, w: (0, j // 2, j % 2, 0, 0))
+    up_keep, up_send = chip_call(
+        functools.partial(up_grad_kernel, block),
+        (steps,),
+        [whole(both, width), wide_spec],
+        [swap_spec, swap_spec],
+        [shaped((2, 2, 2, block, piece), BF)] * 2,
+        scratch=[pltpu.VMEM((width, both), BF)],
+        flops=2 * both * width * inner,
+        moved=5 * 2**20,
+    )(where, normed_two, dbefore)
+    up_got = to_core(up_send)
+
+    def by_core(kept, got):
+        first = core == 0
+        return jnp.stack([jnp.where(first, kept, got), jnp.where(first, got, kept)], axis=2)
+
+    up_blocks = by_core(up_keep, up_got).reshape(2, zs, 2, block, piece)
+    g_w_up = sum_to_owner(up_blocks, at, block // 2)
+
+    dnormed_keep, dnormed_send = chip_call(
+        back_up_kernel,
+        (steps,),
+        [wide_spec, up_spec],
+        [whole(both, width)] * 2,
+        [shaped((both, width), F32), shaped((both, width), BF)],
+        scratch=[pltpu.VMEM((both, width), F32)],
+        flops=2 * both * width * inner,
+        moved=6 * 2**20,
+    )(where, dbefore, w_up)
+    dnormed_got = to_core(dnormed_send)
+
+    feed_keep, feed_send = chip_call(
+        feed_kernel,
+        (steps,),
+        [wide_spec, down_spec],
+        [whole(rows, width)] * 2,
+        [shaped((rows, width), F32), shaped((rows, width), BF)],
+        scratch=[pltpu.VMEM((both, width), F32)],
+        flops=2 * both * width * inner,
+        moved=5 * 2**20,
+    )(where, act, w_down)
+    feed_got = to_core(feed_send)
+    out, scale_two_sum = chip_call(
+        functools.partial(result_kernel, *names),
+        (1,),
+        [whole(rows, width), whole(rows, width), whole(rows, width), whole(rows, width), vec_spec],
+        [whole(rows, width), whole(1, width)],
+        [shaped((rows, width), BF), shaped((1, width), F32)],
+        moved=3 * 2**20,
+    )(where, feed_keep, feed_got, mid, cotangent, vec)
+
+    dmid, dattended, gout, middle_sums = chip_call(
+        functools.partial(middle_kernel, *names),
+        (1,),
+        [whole(both, width)] * 3
+        + [whole(rows, width), whole(rows, width), vec_spec, whole(both, half), whole(half, width), whole(rows, width)],
+        [whole(rows, width), whole(both, half), whole(2, sets, width // sets // 2, half), whole(4, width)],
+        [shaped((rows, width), F32), shaped((both, half), BF), shaped((2, sets, width // sets // 2, half), BF),
+         shaped((4, width), F32)],
+        scratch=[pltpu.VMEM((both, width), BF)],
+        flops=4 * both * width * half,
+        moved=8 * 2**20,
+    )(where, dnormed_keep, dnormed_got, mid, cotangent, cot_sib, vec, attended, w_out_own, branch)
+
+    dquery, dkeys, dvalues = chip_call(
+        functools.partial(attend_grad_kernel, *names),
+        (1,),
+        [whole(both, half), whole(total_rows, half), whole(total_rows, half), whole(both, half), whole(both, half),
+         whole(pairs * tiles, 4 * TILE)],
+        [whole(both, half), whole(total_rows, half), whole(total_rows, half)],
+        [shaped((both, half), BF), shaped((total_rows, half), BF), shaped((total_rows, half), BF)],
+        scratch=[pltpu.VMEM((total_rows, 2 * HEAD_SIZE), F32)] * 2 + [pltpu.VMEM((2 * HEAD_SIZE, 4 * TILE), F32)],
+        flops=10 * both * total_rows * half,
+        moved=6 * 2**20,
+    )(where, query, keys, values, attended, dattended, logsum)
+
+    units = 12
+    unit_rows = 3 * half // units // 2
+    qkv_keep, qkv_send, bias_qv_sum = chip_call(
+        qkv_grad_kernel,
+        (1,),
+        [whole(both, width), whole(both, width), whole(both, half), whole(total_rows, half), whole(total_rows, half)],
+        [whole(2, units, unit_rows, half), whole(2, units, unit_rows, half), whole(2, half)],
+        [shaped((2, units, unit_rows, half), BF)] * 2 + [shaped((2, half), F32)],
+        flops=2 * (both + 2 * total_rows) * width * half,
+        moved=6 * 2**20,
+    )(where, normed_near, normed_far, dquery, dkeys, dvalues)
+    qkv_got = to_core(qkv_send)
+
+    dtok_keep, dtok_send, first_sums = chip_call(
+        tokens_grad_kernel,
+        (1,),
+        [whole(rows, width)] * 4
+        + [whole(both, half), whole(total_rows, half), whole(total_rows, half), whole(width, 3 * half)],
+        [whole(2, rows, width), whole(2, rows, width), whole(2, width)],
+        [shaped((2, rows, width), F32), shaped((2, rows, width), BF), shaped((2, width), F32)],
+        flops=2 * (both + 2 * total_rows) * width * half,
+        moved=8 * 2**20,
+    )(where, tokens, sib, far_a, far_b, dquery, dkeys, dvalues, w_qkv_own)
+    dtok = dtok_keep + to_core(dtok_send).astype(F32)
+    grad_tokens = chip_call(
+        first_norm_grad_kernel,
+        (1,),
+        [whole(rows, width)] * 4 + [vec_spec],
+        whole(rows, width),
+        shaped((rows, width), BF),
+        moved=3 * 2**20,
+    )(where, dtok[0], to_x(dtok[1].astype(BF)), tokens, dmid, vec)
+
+    def placed(halves, groups):
+        cut = halves.reshape(groups, 2, 1, -1)
+        mine = lax.broadcasted_iota(jnp.int32, (1, 1, 2, 1), 2) == core
+        return jnp.where(mine, cut, 0.0).reshape(-1)
+
+    bias_q_sum, bias_v_sum = placed(bias_qv_sum[0:1], 1), placed(bias_qv_sum[1:2], 1)
+    g_vectors = jnp.concatenate(
+        [
+            first_sums.reshape(-1),
+            bias_q_sum,
+            bias_v_sum,
+            middle_sums.reshape(-1),
+            bias_d_sum.reshape(-1),
+            scale_two_sum.reshape(-1),
+            placed(bias_up_sum, 1),
+        ]
+    )
+    share = vectors.shape[0] // (sets * parts)
+    g_vectors = g_vectors.reshape(zs, 2, 2, 2, share)
+    g_vectors = picked(g_vectors, core, 3) + to_core(picked(g_vectors, 1 - core, 3))
+    g_vectors = g_vectors.transpose(2, 0, 1, 3)[:, :, :, None, :].astype(BF)
+    g_vectors = jnp.pad(g_vectors, ((0, 0), (0, 0), (0, 0), (0, 15), (0, half - share)))
+
+    cut = (2, 3, 2, 2, unit_rows, half)
+    qkv_blocks = jnp.stack(
+        [jnp.where(core == 0, qkv_keep.reshape(cut), qkv_got.reshape(cut)),
+         jnp.where(core == 0, qkv_got.reshape(cut), qkv_keep.reshape(cut))], axis=3
+    ).reshape(2, zs, 2, 3 * unit_rows, half)
+    out_blocks = gout.reshape(2, zs, 2, unit_rows, half)
+    last_blocks = jnp.concatenate([qkv_blocks, out_blocks, g_vectors], axis=3)
+    last = sum_to_owner(last_blocks, at, last_blocks.shape[3] // 2)
+    g_w_qkv = unpacked(last[: 3 * unit_rows].reshape(3, unit_rows, half)).T
+    g_w_out = unpacked(last[3 * unit_rows : 4 * unit_rows].reshape(1, unit_rows, half)).T
+    g_vec = last[4 * unit_rows, :share]
+    return (out[None], grad_tokens[None], g_w_qkv, g_w_out, g_w_up, g_w_down, g_vec)
+
+
+def is_aligned(mesh, tokens, w_up):
+    parts, sets = mesh.shape["blk"], mesh.shape["dp"]
+    width, hidden = w_up.shape
+    rows = tokens.shape[1] // parts
+    return (
+        parts == 4
+        and sets == 2 * parts
+        and rows % TILE == 0
+        and (hidden // sets) % 128 == 0
+        and (width // 2) % 128 == 0
+        and (width // sets) % 32 == 0
+        and width == H * HEAD_SIZE
+    )
+
+
 def solution(mesh):
-    return jax.shard_map(
-        on_device,
-        mesh=mesh,
-        in_specs=(
-            P("dp", "blk", None),
-            P("dp", None),
-            P(),
-            P(),
-            P(),
-            P(),
-            P(),
-            P("dp", "blk", None),
-        ),
-        out_specs=(
-            P("dp", "blk", None),
-            P("dp", "blk", None),
-            P("blk", "dp"),
-            P("blk", "dp"),
-            P("blk", "dp"),
-            P("blk", "dp"),
-            P(("dp", "blk")),
-        ),
-        check_vma=False,
-    )
+    def run(tokens, lengths, w_qkv, w_out, w_up, w_down, vectors, cotangent):
+        body = on_device_aligned if is_aligned(mesh, tokens, w_up) else on_device
+        return jax.shard_map(
+            body,
+            mesh=mesh,
+            in_specs=(
+                P("dp", "blk", None),
+                P("dp", None),
+                P(),
+                P(),
+                P(),
+                P(),
+                P(),
+                P("dp", "blk", None),
+            ),
+            out_specs=(
+                P("dp", "blk", None),
+                P("dp", "blk", None),
+                P("blk", "dp"),
+                P("blk", "dp"),
+                P("blk", "dp"),
+                P("blk", "dp"),
+                P(("dp", "blk")),
+            ),
+            check_vma=False,
+        )(tokens, lengths, w_qkv, w_out, w_up, w_down, vectors, cotangent)
+
+    return run

time: 652 us -> 232 us (0.36)
  waiting for transfers between devices: 323 us -> 61.8 us
  matrix products: 107 us -> 0 us
  Pallas kernels: 0 us -> 75.6 us
  other arithmetic: 61.7 us -> 11.9 us
  local copies, waits for them, and re-layouts: 89 us -> 43 us
  blocking collectives: 43.3 us -> 0 us
  starting transfers between devices: 7.92 us -> 37 us
  between operations: 16.1 us -> 1.63 us
    reduce_scatter x5 -> x0, waiting for transfers between devices: 162 us -> none  [the longest x1 87.4 us: on_device(): lax.psum_scatter(g_w_down.astype(jnp.bfloat16), 'dp', scatter_dimension=1...]
    dot_general x36 -> x0, matrix products: 107 us -> none  [the longest x4 15.1 us: contract_rows(): lax.dot_general(left, right, (((0,), (0,)), ((), ())), preferred_element_...]
    unnamed x13 -> x0, waiting for transfers between devices: 97 us -> none
    pallas_call x0 -> x13, Pallas kernels: none -> 75.6 us  [the longest x1 12.5 us: on_device_aligned(): chip_call(functools.partial(attend_kernel, *names), (1,), [whole(rows, wi...]
    unnamed x2 -> x0, blocking collectives: 43.3 us -> none
    all_gather x2 -> x0, waiting for transfers between devices: 31.2 us -> none  [the longest x1 21.8 us: on_device(): lax.all_gather(values, 'blk', axis=0, tiled=True)]
    ppermute x14 -> x33, starting transfers between devices: 7.51 us -> 37 us  [the longest x9 18.2 us: along_z(): lax.ppermute(array, 'dp', [(i, (i + 2 * by) % length) for i in range(leng...]
    ppermute x14 -> x33, waiting for transfers between devices: 32.9 us -> 61.8 us  [the longest x8 29.2 us: to_x(): return lax.ppermute(array, 'blk', [(i, i ^ 2) for i in range(length)])]
  transfers between devices with their start and end apart: 24 -> 33, of which waited for: 20 -> 12; matrix products, arithmetic and copies ran while one was open for 23% -> 13% of each run, Pallas kernels for 0% -> 28%
where the time goes in v1:
time: 232 us; the launch traced here: 231 us
  Pallas kernels  75.6 us (33%)
  waiting for transfers between devices  61.8 us (27%)
  local copies, waits for them, and re-layouts  43 us (19%)
  starting transfers between devices  37 us (16%)
  other arithmetic  11.9 us (5%)
    ppermute x8, waiting for transfers between devices, to_x(): return lax.ppermute(array, 'blk', [(i, i ^ 2) for i in range(length)])  29.2 us
    unnamed x111, local copies, waits for them, and re-layouts  26.7 us
    ppermute x9, waiting for transfers between devices, along_z(): lax.ppermute(array, 'dp', [(i, (i + 2 * by) % length) for i in range(leng...  21.8 us
    ppermute x9, starting transfers between devices, along_z(): lax.ppermute(array, 'dp', [(i, (i + 2 * by) % length) for i in range(leng...  18.2 us
    pallas_call x1, Pallas kernels, on_device_aligned(): chip_call(functools.partial(attend_kernel, *names), (1,), [whole(rows, wi...  12.5 us
    pallas_call x1, Pallas kernels, on_device_aligned(): chip_call(functools.partial(attend_grad_kernel, *names), (1,), [whole(bot...  11 us
    ppermute x8, starting transfers between devices, to_x(): return lax.ppermute(array, 'blk', [(i, i ^ 2) for i in range(length)])  10.9 us
    ppermute x6, waiting for transfers between devices, to_y(): return lax.ppermute(array, 'dp', [(i, i ^ 1) for i in range(length)])  10.8 us
  transfers between devices with their start and end apart: 33, of which 12 were waited for; matrix products, arithmetic and copies ran while one was open for 13% of the time, Pallas kernels for 28%

profile of v1, /device:TPU:0, one launch (start us, length us, event | category | flops | bytes accessed | tf_op | source)
XLA Modules:
  0.0 230.9 jit_solution(260837787526898107)
XLA Ops:
  0.6 3.0 %collective-permute-start = (bf16[256,768]{1,0:T(8,128)(2,1)}, bf16[256,768]{1,0:T(8,128)(2,1)S(1)}, u32[]{:S(2)}, u32[]{:S(2)}) collective-permute-start(bf16[256,768]{1,0:T(8,128)(2,1)} %bitcast.175), channel_id=1, source_target_pairs={{0,2},{1,3},{2,0},{3,1},{4,6},{5,7},{6,4},{7,5},{8,10},{9,11},{10,... | collective-permute-start | bytes 1179656 | tf_op jit(solution)/shard_map/ppermute | solution.py:770
  3.6 9.3 %collective-permute-done.far_a_ref = bf16[256,768]{1,0:T(8,128)(2,1)S(1)} collective-permute-done((bf16[256,768]{1,0:T(8,128)(2,1)}, bf16[256,768]{1,0:T(8,128)(2,1)S(1)}, u32[]{:S(2)}, u32[]{:S(2)}) %collective-permute-start) | collective-permute-done | bytes 393248 | tf_op jit(solution)/shard_map/ppermute | solution.py:770
  14.2 5.8 %copy.39 = bf16[768,2304]{0,1:T(8,128)(2,1)} copy(bf16[768,2304]{1,0:T(8,128)(2,1)} %param.10) | data formatting | bytes 7077888 | tf_op args[2]
  20.0 2.8 %constant_dynamic-slice_fusion.11 = bf16[768,3,2,1,192]{0,4,3,2,1:T(8,128)(2,1)} fusion(bf16[768,3,2,2,192]{0,4,3,2,1:T(8,128)(2,1)} %bitcast.184, s32[]{:T(128)S(6)} %select_n.202), kind=kLoop, calls=%fused_computation.125 | loop fusion | bytes 3538948 | tf_op jit(solution)/shard_map/jit(dynamic_index_in_dim)/dynamic_slice | solution.py:784
  22.8 2.8 %copy.41.weight_ref = bf16[768,1152]{1,0:T(8,128)(2,1)S(1)} copy(bf16[768,1152]{0,1:T(8,128)(2,1)} %bitcast.185) | data formatting | bytes 3538944 | tf_op jit(solution)/shard_map/reshape | solution.py:843
  26.1 3.1 %shard_map.135 = (bf16[512,768]{1,0:T(8,128)(2,1)S(1)}, bf16[512,384]{1,0:T(8,128)(2,1)S(1)}, bf16[512,384]{1,0:T(8,128)(2,1)S(1)}, bf16[512,384]{1,0:T(8,128)(2,1)S(1)}) custom-call(s32[9]{0:T(128)S(1)} %concatenate.18.where_ref, bf16[256,768]{1,0:T(8,128)(2,1)S(1)} %bitcast.177, bf16[256,768]{1,0:T(8,128)(2,1)} %collective-permute-done.2.sib_ref, ...), custom_call_target="tpu_custom_call" | custom-call | flops 905969664 | bytes 4194304 | tf_op jit(solution)/shard_map/pallas_call | solution.py:856
  30.1 12.5 %shard_map.136 = (bf16[512,768]{1,0:T(8,128)(2,1)S(1)}, bf16[1024,384]{1,0:T(8,128)(2,1)S(1)}, bf16[1024,384]{1,0:T(8,128)(2,1)S(1)}, bf16[512,384]{1,0:T(8,128)(2,1)S(1)}, f32[12,256]{1,0:T(8,128)S(1)}) custom-call(s32[9]{0:T(128)S(1)} %concatenate.18.where_ref, bf16[256,768]{1,0:T(8,128)(2,1)S(1)} %collective-permute-done.far_a_ref, ...), custom_call_target="tpu_custom_call" | custom-call | flops 1409286144 | bytes 8388608 | tf_op jit(solution)/shard_map/pallas_call | solution.py:879
  45.6 1.4 constant_dynamic-slice_fusion.8
  47.0 5.1 %shard_map.137 = (bf16[512,1536]{1,0:T(8,128)(2,1)S(1)}, bf16[768,512]{1,0:T(8,128)(2,1)S(1)}, f32[1,768]{1,0:T(1,128)S(1)}) custom-call(s32[9]{0:T(128)S(1)} %concatenate.18.where_ref, bf16[256,768]{1,0:T(8,128)(2,1)S(1)} %bitcast.168, bf16[256,768]{1,0:T(8,128)(2,1)S(1)} %collective-permute-done.4.sib_ref, f32[10,768]{1,0:T(8,128)S(1)} %slice.83.vec_ref, ...), custom_call_target="tpu_custom_call" | custom-call | flops 1207959552 | bytes 5242880 | tf_op jit(solution)/shard_map/pallas_call | solution.py:866
  52.1 1.1 copy-done.21
  55.4 10.2 %shard_map.138 = (bf16[512,1536]{1,0:T(8,128)(2,1)}, bf16[512,1536]{1,0:T(8,128)(2,1)}, bf16[2,768,768]{2,1,0:T(8,128)(2,1)}, f32[512,768]{1,0:T(8,128)}, f32[25...) custom-call(s32[9]{0:T(128)S(1)} %concatenate.18.where_ref, ...), custom_call_target="tpu_custom_call" | custom-call | flops 3019898880 | bytes 12582912 | tf_op jit(solution)/shard_map/pallas_call | solution.py:893
  65.5 2.1 fusion.49
  68.6 1.8 collective-permute-start.28
  72.1 1.5 collective-permute-start.26
  73.6 5.8 %shard_map.139 = (f32[256,768]{1,0:T(8,128)S(1)}, bf16[256,768]{1,0:T(8,128)(2,1)}) custom-call(s32[9]{0:T(128)S(1)} %concatenate.18.where_ref, bf16[512,1536]{1,0:T(8,128)(2,1)S(1)} %copy-done.4, bf16[3072,768]{1,0:T(8,128)(2,1)} %down_ref.3), custom_call_target="tpu_custom_call" | custom-call | flops 1207959552 | bytes 5242880 | tf_op jit(solution)/shard_map/pallas_call | solution.py:945
  80.2 4.3 %shard_map.147 = (bf16[2,2,2,192,384]{4,3,2,1,0:T(8,128)(2,1)S(1)}, bf16[2,2,2,192,384]{4,3,2,1,0:T(8,128)(2,1)}) custom-call(s32[9]{0:T(128)S(1)} %concatenate.18.where_ref, bf16[512,768]{1,0:T(8,128)(2,1)S(1)} %get-tuple-element.83.normed_ref, bf16[512,1536]{1,0:T(8,128)(2,1)S(1)} %copy-done.3), custom_call_target="tpu_custom_call" | custom-call | flops 1207959552 | bytes 5242880 | tf_op jit(solution)/shard_map/pallas_call | solution.py:914
  86.1 5.9 %shard_map.141 = (f32[512,768]{1,0:T(8,128)S(1)}, bf16[512,768]{1,0:T(8,128)(2,1)}) custom-call(s32[9]{0:T(128)S(1)} %concatenate.18.where_ref, bf16[512,1536]{1,0:T(8,128)(2,1)S(1)} %copy-done.3, bf16[768,3072]{1,0:T(8,128)(2,1)} %up_ref.3), custom_call_target="tpu_custom_call" | custom-call | flops 1207959552 | bytes 6291456 | tf_op jit(solution)/shard_map/pallas_call | solution.py:933
  94.4 2.6 %shard_map.140 = (bf16[256,768]{1,0:T(8,128)(2,1)}, f32[1,768]{1,0:T(1,128)S(1)}) custom-call(s32[9]{0:T(128)S(1)} %concatenate.18.where_ref, f32[256,768]{1,0:T(8,128)S(1)} %copy-done.13, bf16[256,768]{1,0:T(8,128)(2,1)} %collective-permute-done.5.got_ref, f32[512,768]{1,0:T(8,128)S(1)} %copy-done, bf16[256,768]{1,0:T(8,128)(2,1)S(1)} %bitcast.169, ...), custom_call_target="tpu_custom_call" | custom-call | bytes 3145728 | tf_op jit(solution)/shard_map/pallas_call | solution.py:956
  97.1 1.4 fusion.4
  99.9 1.2 fusion.5
  102.3 5.1 %shard_map.142 = (f32[256,768]{1,0:T(8,128)S(1)}, bf16[512,384]{1,0:T(8,128)(2,1)S(1)}, bf16[2,8,48,384]{3,2,1,0:T(8,128)(2,1)S(1)}, f32[4,768]{1,0:T(4,128)S(1)}) custom-call(s32[9]{0:T(128)S(1)} %concatenate.18.where_ref, f32[512,768]{1,0:T(8,128)} %copy-done.5, bf16[512,768]{1,0:T(8,128)(2,1)} %collective-permute-done.6.got_ref, ...), custom_call_target="tpu_custom_call" | custom-call | flops 603979776 | bytes 8388608 | tf_op jit(solution)/shard_map/pallas_call | solution.py:965
  109.1 11.0 %shard_map.143 = (bf16[512,384]{1,0:T(8,128)(2,1)S(1)}, bf16[1024,384]{1,0:T(8,128)(2,1)S(1)}, bf16[1024,384]{1,0:T(8,128)(2,1)S(1)}) custom-call(s32[9]{0:T(128)S(1)} %concatenate.18.where_ref, bf16[512,384]{1,0:T(8,128)(2,1)S(1)} %copy-done.36, bf16[1024,384]{1,0:T(8,128)(2,1)S(1)} %copy-done.40, bf16[1024,384]{1,0:T(8,128)(2,1)S(1)} %copy-done.42, ...), custom_call_target="tpu_custom_call" | custom-call | flops 2013265920 | bytes 6291456 | tf_op jit(solution)/shard_map/pallas_call | solution.py:978
  120.3 3.4 %shard_map.146 = (bf16[2,12,48,384]{3,2,1,0:T(8,128)(2,1)S(1)}, bf16[2,12,48,384]{3,2,1,0:T(8,128)(2,1)}, f32[2,384]{1,0:T(2,128)S(1)}) custom-call(s32[9]{0:T(128)S(1)} %concatenate.18.where_ref, bf16[512,768]{1,0:T(8,128)(2,1)S(1)} %copy-done.34, bf16[512,768]{1,0:T(8,128)(2,1)S(1)} %copy-done.38, bf16[512,384]{1,0:T(8,128)(2,1)S(1)} %get-tuple-element.66.dquery_ref, ...), custom_call_target="tpu_custom_call" | custom-call | flops 1509949440 | bytes 6291456 | tf_op jit(solution)/shard_map/pallas_call | solution.py:992
  128.2 4.9 %shard_map.144 = (f32[2,256,768]{2,1,0:T(8,128)S(1)}, bf16[2,256,768]{2,1,0:T(8,128)(2,1)S(1)}, f32[2,768]{1,0:T(2,128)S(1)}) custom-call(s32[9]{0:T(128)S(1)} %concatenate.18.where_ref, bf16[256,768]{1,0:T(8,128)(2,1)S(1)} %bitcast.179, bf16[256,768]{1,0:T(8,128)(2,1)} %collective-permute-done.2.sib_ref, bf16[256,768]{1,0:T(8,128)(2,1)S(1)} %copy-done.26, ...), custom_call_target="tpu_custom_call" | custom-call | flops 1509949440 | bytes 8388608 | tf_op jit(solution)/shard_map/pallas_call | solution.py:1003
  136.3 1.8 collective-permute-start.30
  138.1 2.6 %collective-permute-start.31 = (bf16[96,768]{1,0:T(8,128)(2,1)S(1)}, bf16[96,768]{1,0:T(8,128)(2,1)S(1)}, u32[]{:S(2)}, u32[]{:S(2)}) collective-permute-start(bf16[96,768]{1,0:T(8,128)(2,1)S(1)} %get-tuple-element.125), channel_id=1, source_target_pairs={{0,16},{4,20},{8,24},{12,28},{16,0},{20,4},{24,8},{28,12},{1,17},{... | collective-permute-start | bytes 442376 | tf_op jit(solution)/shard_map/ppermute | solution.py:780
  140.8 1.3 collective-permute-start.32
  142.1 2.8 %collective-permute-done.30 = bf16[96,768]{1,0:T(8,128)(2,1)S(1)} collective-permute-done((bf16[96,768]{1,0:T(8,128)(2,1)S(1)}, bf16[96,768]{1,0:T(8,128)(2,1)S(1)}, u32[]{:S(2)}, u32[]{:S(2)}) %collective-permute-start.30) | collective-permute-done | bytes 147488 | tf_op jit(solution)/shard_map/ppermute | solution.py:780
  145.0 5.7 %collective-permute-done.31 = bf16[96,768]{1,0:T(8,128)(2,1)S(1)} collective-permute-done((bf16[96,768]{1,0:T(8,128)(2,1)S(1)}, bf16[96,768]{1,0:T(8,128)(2,1)S(1)}, u32[]{:S(2)}, u32[]{:S(2)}) %collective-permute-start.31) | collective-permute-done | bytes 147488 | tf_op jit(solution)/shard_map/ppermute | solution.py:780
  151.4 1.5 select_bitcast_fusion.1
  153.8 1.6 collective-permute-start.21
  155.6 1.5 collective-permute-start.19
  158.5 1.3 broadcast_select_fusion.1
  161.8 8.3 %collective-permute-done.21 = bf16[2,4,96,384]{3,2,1,0:T(8,128)(2,1)S(1)} collective-permute-done((bf16[2,4,96,384]{3,2,1,0:T(8,128)(2,1)S(1)}, bf16[2,4,96,384]{3,2,1,0:T(8,128)(2,1)S(1)}, u32[]{:S(2)}, u32[]{:S(2)}) %collective-permute-start.21) | collective-permute-done | bytes 589856 | tf_op jit(solution)/shard_map/ppermute | solution.py:775
  170.3 1.5 collective-permute-start.22
  172.1 1.5 collective-permute-start.20
  174.4 5.9 %collective-permute-done.8.got_ref = bf16[256,768]{1,0:T(8,128)(2,1)S(1)} collective-permute-done((bf16[256,768]{1,0:T(8,128)(2,1)S(1)}, bf16[256,768]{1,0:T(8,128)(2,1)S(1)}, u32[]{:S(2)}, u32[]{:S(2)}) %collective-permute-start.8) | collective-permute-done | bytes 393248 | tf_op jit(solution)/shard_map/ppermute | solution.py:770
  180.3 1.9 shard_map.145
  182.2 4.5 %collective-permute-done.22 = bf16[4,96,384]{2,1,0:T(8,128)(2,1)S(1)} collective-permute-done((bf16[4,96,384]{2,1,0:T(8,128)(2,1)S(1)}, bf16[4,96,384]{2,1,0:T(8,128)(2,1)S(1)}, u32[]{:S(2)}, u32[]{:S(2)}) %collective-permute-start.22) | collective-permute-done | bytes 294944 | tf_op jit(solution)/shard_map/ppermute | solution.py:770
  186.7 2.3 collective-permute-done.20
  189.4 1.5 collective-permute-start.14
  190.9 9.4 %collective-permute-done.10 = bf16[4,2,104,384]{3,2,0,1:T(8,128)(2,1)S(1)} collective-permute-done((bf16[4,2,104,384]{3,2,0,1:T(8,128)(2,1)S(1)}, bf16[4,2,104,384]{3,2,0,1:T(8,128)(2,1)S(1)}, u32[]{:S(2)}, u32[]{:S(2)}) %collective-permute-start.10) | collective-permute-done | bytes 639008 | tf_op jit(solution)/shard_map/ppermute | solution.py:770
  201.2 3.7 %collective-permute-start.23 = (bf16[192,384]{1,0:T(8,128)(2,1)S(1)}, bf16[192,384]{1,0:T(8,128)(2,1)S(1)}, u32[]{:S(2)}, u32[]{:S(2)}) collective-permute-start(bf16[192,384]{1,0:T(8,128)(2,1)S(1)} %get-tuple-element.127), channel_id=1, source_target_pairs={{0,8},{4,12},{8,16},{12,20},{16,24},{20,28},{24,0},{28,4},{1,9},{5... | collective-permute-start | bytes 442376 | tf_op jit(solution)/shard_map/ppermute | solution.py:780
  204.9 1.7 collective-permute-start.24
  207.8 3.7 %collective-permute-start.15 = (bf16[208,384]{1,0:T(8,128)(2,1)S(1)}, bf16[208,384]{1,0:T(8,128)(2,1)S(1)}, u32[]{:S(2)}, u32[]{:S(2)}) collective-permute-start(bf16[208,384]{1,0:T(8,128)(2,1)S(1)} %get-tuple-element.121), channel_id=1, source_target_pairs={{0,8},{4,12},{8,16},{12,20},{16,24},{20,28},{24,0},{28,4},{1,9},{5... | collective-permute-start | bytes 479240 | tf_op jit(solution)/shard_map/ppermute | solution.py:780
  211.5 1.6 collective-permute-start.16
  214.1 5.5 %collective-permute-done.24 = bf16[192,384]{1,0:T(8,128)(2,1)S(1)} collective-permute-done((bf16[192,384]{1,0:T(8,128)(2,1)S(1)}, bf16[192,384]{1,0:T(8,128)(2,1)S(1)}, u32[]{:S(2)}, u32[]{:S(2)}) %collective-permute-start.24) | collective-permute-done | bytes 147488 | tf_op jit(solution)/shard_map/ppermute | solution.py:780
  220.5 7.7 %collective-permute-done.16 = bf16[208,384]{1,0:T(8,128)(2,1)S(1)} collective-permute-done((bf16[208,384]{1,0:T(8,128)(2,1)S(1)}, bf16[208,384]{1,0:T(8,128)(2,1)S(1)}, u32[]{:S(2)}, u32[]{:S(2)}) %collective-permute-start.16) | collective-permute-done | bytes 159776 | tf_op jit(solution)/shard_map/ppermute | solution.py:780
  (226 shorter events, 40.4 us)
Async XLA Ops:
  0.6 12.3 %collective-permute-start = (bf16[256,768]{1,0:T(8,128)(2,1)}, bf16[256,768]{1,0:T(8,128)(2,1)S(1)}, u32[]{:S(2)}, u32[]{:S(2)}) collective-permute-start(bf16[256,768]{1,0:T(8,128)(2,1)} %bitcast.175), channel_id=1, source_target_pairs={{0,2},{1,3},{2,0},{3,1},{4,6},{5,7},{6,4},{7,5},{8,10},{9,11},{10,... | collective-permute-start | bytes 1179656 | tf_op jit(solution)/shard_map/ppermute | solution.py:770
  3.6 22.5 %collective-permute-start.2 = (bf16[256,768]{1,0:T(8,128)(2,1)}, bf16[256,768]{1,0:T(8,128)(2,1)}, u32[]{:S(2)}, u32[]{:S(2)}) collective-permute-start(bf16[256,768]{1,0:T(8,128)(2,1)} %bitcast.176), channel_id=1, source_target_pairs={{0,1},{1,0},{2,3},{3,2},{4,5},{5,4},{6,7},{7,6},{8,9},{9,8},{10,11... | collective-permute-start | bytes 1179656 | tf_op jit(solution)/shard_map/ppermute | solution.py:765
  13.0 17.2 %copy-start.25 = (bf16[256,768]{1,0:T(8,128)(2,1)}, bf16[256,768]{1,0:T(8,128)(2,1)S(1)}, u32[]{:S(2)}) copy-start(bf16[256,768]{1,0:T(8,128)(2,1)S(1)} %collective-permute-done.far_a_ref) | copy-start | bytes 1179652
  13.0 17.2 %collective-permute-start.1 = (bf16[256,768]{1,0:T(8,128)(2,1)S(1)}, bf16[256,768]{1,0:T(8,128)(2,1)}, u32[]{:S(2)}, u32[]{:S(2)}) collective-permute-start(bf16[256,768]{1,0:T(8,128)(2,1)S(1)} %collective-permute-done.far_a_ref), channel_id=1, source_target_pairs={{0,1},{1,0},{2,3},{3,2},{4,5},{5,4},{6,7},{7,6},{8,9},{9,8},{10,11... | collective-permute-start | bytes 1179656 | tf_op jit(solution)/shard_map/ppermute | solution.py:765
  13.0 34.0 %collective-permute-start.4 = (bf16[256,768]{1,0:T(8,128)(2,1)}, bf16[256,768]{1,0:T(8,128)(2,1)S(1)}, u32[]{:S(2)}, u32[]{:S(2)}) collective-permute-start(bf16[256,768]{1,0:T(8,128)(2,1)} %bitcast.167), channel_id=1, source_target_pairs={{0,1},{1,0},{2,3},{3,2},{4,5},{5,4},{6,7},{7,6},{8,9},{9,8},{10,11... | collective-permute-start | bytes 1179656 | tf_op jit(solution)/shard_map/ppermute | solution.py:765
  30.1 12.5 %copy-start.35 = (bf16[512,384]{1,0:T(8,128)(2,1)}, bf16[512,384]{1,0:T(8,128)(2,1)S(1)}, u32[]{:S(2)}) copy-start(bf16[512,384]{1,0:T(8,128)(2,1)S(1)} %get-tuple-element.47.query_ref) | copy-start | bytes 1179652
  30.1 15.3 %copy-start.47 = (f32[10752]{0:T(1024)S(1)}, f32[10752]{0:T(1024)}, u32[]{:S(2)}) copy-start(f32[10752]{0:T(1024)} %param.14) | copy-start | bytes 129028
  45.4 8.8 %copy-start.19 = (bf16[512,384]{1,0:T(8,128)(2,1)}, bf16[512,384]{1,0:T(8,128)(2,1)S(1)}, u32[]{:S(2)}) copy-start(bf16[512,384]{1,0:T(8,128)(2,1)S(1)} %get-tuple-element.50.att_own_ref.att_ref.attended_ref) | copy-start | bytes 1179652
  45.4 8.8 %collective-permute-start.3 = (bf16[512,384]{1,0:T(8,128)(2,1)S(1)}, bf16[512,384]{1,0:T(8,128)(2,1)S(1)}, u32[]{:S(2)}, u32[]{:S(2)}) collective-permute-start(bf16[512,384]{1,0:T(8,128)(2,1)S(1)} %get-tuple-element.50.att_own_ref.att_ref.attended_ref), channel_id=1, source_target_pairs={{0,1},{1,0},{2,3},{3,2},{4,5},{5,4},{6,7},{7,6},{8,9},{9,8},{10,11... | collective-permute-start | bytes 1179656 | tf_op jit(solution)/shard_map/ppermute | solution.py:765
  67.6 11.8 %copy-start.43 = (bf16[2,4,2,48,768]{4,3,2,1,0:T(8,128)(2,1)}, bf16[2,4,2,48,768]{4,3,2,1,0:T(8,128)(2,1)S(1)}, u32[]{:S(2)}) copy-start(bf16[2,4,2,48,768]{4,3,2,1,0:T(8,128)(2,1)S(1)} %get-tuple-element.103) | copy-start | bytes 3538948
  68.6 28.5 %collective-permute-start.28 = (bf16[2,4,48,768]{3,2,1,0:T(8,128)(2,1)}, bf16[2,4,48,768]{3,2,1,0:T(8,128)(2,1)}, u32[]{:S(2)}, u32[]{:S(2)}) collective-permute-start(bf16[2,4,48,768]{3,2,1,0:T(8,128)(2,1)} %dynamic-slice_bitcast_fusion.1), channel_id=1, source_target_pairs={{0,4},{4,0},{8,12},{12,8},{16,20},{20,16},{24,28},{28,24},{1,5},{5... | collective-permute-start | bytes 1769480 | tf_op jit(solution)/shard_map/ppermute | solution.py:775
  72.1 27.9 %collective-permute-start.26 = (bf16[4,2,48,768]{3,2,0,1:T(8,128)(2,1)}, bf16[4,2,48,768]{3,2,0,1:T(8,128)(2,1)}, u32[]{:S(2)}, u32[]{:S(2)}) collective-permute-start(bf16[4,2,48,768]{3,2,0,1:T(8,128)(2,1)} %bitcast.164), channel_id=1, source_target_pairs={{0,2},{1,3},{2,0},{3,1},{4,6},{5,7},{6,4},{7,5},{8,10},{9,11},{10,... | collective-permute-start | bytes 1769480 | tf_op jit(solution)/shard_map/ppermute | solution.py:770
  73.6 6.7 %copy-start.3 = (bf16[512,1536]{1,0:T(8,128)(2,1)S(1)}, bf16[512,1536]{1,0:T(8,128)(2,1)}, u32[]{:S(2)}) copy-start(bf16[512,1536]{1,0:T(8,128)(2,1)} %get-tuple-element.60.dbefore_ref) | copy-start | bytes 4718596
  80.2 13.0 %collective-permute-start.5 = (bf16[256,768]{1,0:T(8,128)(2,1)}, bf16[256,768]{1,0:T(8,128)(2,1)}, u32[]{:S(2)}, u32[]{:S(2)}) collective-permute-start(bf16[256,768]{1,0:T(8,128)(2,1)} %get-tuple-element.55), channel_id=1, source_target_pairs={{0,1},{1,0},{2,3},{3,2},{4,5},{5,4},{6,7},{7,6},{8,9},{9,8},{10,11... | collective-permute-start | bytes 1179656 | tf_op jit(solution)/shard_map/ppermute | solution.py:765
  85.6 7.7 %copy-start = (f32[512,768]{1,0:T(8,128)S(1)}, f32[512,768]{1,0:T(8,128)}, u32[]{:S(2)}) copy-start(f32[512,768]{1,0:T(8,128)} %get-tuple-element.56.mid_ref) | copy-start | bytes 4718596
  85.6 65.8 %collective-permute-start.18 = (bf16[2,2,2,192,384]{4,3,2,1,0:T(8,128)(2,1)}, bf16[2,2,2,192,384]{4,3,2,1,0:T(8,128)(2,1)}, u32[]{:S(2)}, u32[]{:S(2)}) collective-permute-start(bf16[2,2,2,192,384]{4,3,2,1,0:T(8,128)(2,1)} %get-tuple-element.85), channel_id=1, source_target_pairs={{0,1},{1,0},{2,3},{3,2},{4,5},{5,4},{6,7},{7,6},{8,9},{9,8},{10,11... | collective-permute-start | bytes 3538952 | tf_op jit(solution)/shard_map/ppermute | solution.py:765
  93.1 9.1 %collective-permute-start.6 = (bf16[512,768]{1,0:T(8,128)(2,1)}, bf16[512,768]{1,0:T(8,128)(2,1)}, u32[]{:S(2)}, u32[]{:S(2)}) collective-permute-start(bf16[512,768]{1,0:T(8,128)(2,1)} %get-tuple-element.62), channel_id=1, source_target_pairs={{0,1},{1,0},{2,3},{3,2},{4,5},{5,4},{6,7},{7,6},{8,9},{9,8},{10,11... | collective-permute-start | bytes 2359304 | tf_op jit(solution)/shard_map/ppermute | solution.py:765
  99.4 34.6 %collective-permute-start.29 = (bf16[4,48,768]{2,1,0:T(8,128)(2,1)}, bf16[4,48,768]{2,1,0:T(8,128)(2,1)}, u32[]{:S(2)}, u32[]{:S(2)}) collective-permute-start(bf16[4,48,768]{2,1,0:T(8,128)(2,1)} %dynamic-slice_bitcast_fusion.5), channel_id=1, source_target_pairs={{0,2},{1,3},{2,0},{3,1},{4,6},{5,7},{6,4},{7,5},{8,10},{9,11},{10,... | collective-permute-start | bytes 884744 | tf_op jit(solution)/shard_map/ppermute | solution.py:770
  101.1 6.2 %copy-start.44 = (bf16[4,2,48,768]{3,2,0,1:T(8,128)(2,1)}, bf16[4,2,48,768]{3,2,0,1:T(8,128)(2,1)S(1)}, u32[]{:S(2)}) copy-start(bf16[4,2,48,768]{3,2,0,1:T(8,128)(2,1)S(1)} %fusion.5) | copy-start | bytes 1769476
  101.9 33.2 %collective-permute-start.27 = (bf16[4,48,768]{2,1,0:T(8,128)(2,1)}, bf16[4,48,768]{2,1,0:T(8,128)(2,1)}, u32[]{:S(2)}, u32[]{:S(2)}) collective-permute-start(bf16[4,48,768]{2,1,0:T(8,128)(2,1)} %dynamic-slice_bitcast_fusion.6), channel_id=1, source_target_pairs={{0,4},{4,0},{8,12},{12,8},{16,20},{20,16},{24,28},{28,24},{1,5},{5... | collective-permute-start | bytes 884744 | tf_op jit(solution)/shard_map/ppermute | solution.py:775
  102.3 6.8 %copy-start.36 = (bf16[512,384]{1,0:T(8,128)(2,1)S(1)}, bf16[512,384]{1,0:T(8,128)(2,1)}, u32[]{:S(2)}) copy-start(bf16[512,384]{1,0:T(8,128)(2,1)} %copy-done.35) | copy-start | bytes 1179652
  102.3 6.8 %copy-start.40 = (bf16[1024,384]{1,0:T(8,128)(2,1)S(1)}, bf16[1024,384]{1,0:T(8,128)(2,1)}, u32[]{:S(2)}) copy-start(bf16[1024,384]{1,0:T(8,128)(2,1)} %copy-done.39) | copy-start | bytes 2359300
  102.3 6.8 %copy-start.42 = (bf16[1024,384]{1,0:T(8,128)(2,1)S(1)}, bf16[1024,384]{1,0:T(8,128)(2,1)}, u32[]{:S(2)}) copy-start(bf16[1024,384]{1,0:T(8,128)(2,1)} %copy-done.41) | copy-start | bytes 2359300
  109.1 11.1 %copy-start.34 = (bf16[512,768]{1,0:T(8,128)(2,1)S(1)}, bf16[512,768]{1,0:T(8,128)(2,1)}, u32[]{:S(2)}) copy-start(bf16[512,768]{1,0:T(8,128)(2,1)} %copy-done.33) | copy-start | bytes 2359300
  109.1 11.1 %copy-start.38 = (bf16[512,768]{1,0:T(8,128)(2,1)S(1)}, bf16[512,768]{1,0:T(8,128)(2,1)}, u32[]{:S(2)}) copy-start(bf16[512,768]{1,0:T(8,128)(2,1)} %copy-done.37) | copy-start | bytes 2359300
  124.5 33.5 %collective-permute-start.9 = (bf16[2,12,48,384]{3,2,1,0:T(8,128)(2,1)}, bf16[2,12,48,384]{3,2,1,0:T(8,128)(2,1)}, u32[]{:S(2)}, u32[]{:S(2)}) collective-permute-start(bf16[2,12,48,384]{3,2,1,0:T(8,128)(2,1)} %get-tuple-element.75), channel_id=1, source_target_pairs={{0,1},{1,0},{2,3},{3,2},{4,5},{5,4},{6,7},{7,6},{8,9},{9,8},{10,11... | collective-permute-start | bytes 2654216 | tf_op jit(solution)/shard_map/ppermute | solution.py:765
  133.4 7.3 %collective-permute-start.12 = (f32[4,2,2,336]{3,2,1,0:T(2,128)S(1)}, f32[4,2,2,336]{3,2,1,0:T(2,128)S(1)}, u32[]{:S(2)}, u32[]{:S(2)}) collective-permute-start(f32[4,2,2,336]{3,2,1,0:T(2,128)S(1)} %bitcast.197), channel_id=1, source_target_pairs={{0,1},{1,0},{2,3},{3,2},{4,5},{5,4},{6,7},{7,6},{8,9},{9,8},{10,11... | collective-permute-start | bytes 64520 | tf_op jit(solution)/shard_map/ppermute | solution.py:765
  136.3 15.1 %copy-start.7 = (bf16[2,2,2,192,384]{4,3,2,1,0:T(8,128)(2,1)S(1)}, bf16[2,2,2,192,384]{4,3,2,1,0:T(8,128)(2,1)}, u32[]{:S(2)}) copy-start(bf16[2,2,2,192,384]{4,3,2,1,0:T(8,128)(2,1)} %copy-done.6) | copy-start | bytes 3538948
  136.3 8.6 %collective-permute-start.30 = (bf16[96,768]{1,0:T(8,128)(2,1)S(1)}, bf16[96,768]{1,0:T(8,128)(2,1)S(1)}, u32[]{:S(2)}, u32[]{:S(2)}) collective-permute-start(bf16[96,768]{1,0:T(8,128)(2,1)S(1)} %get-tuple-element.124), channel_id=1, source_target_pairs={{0,8},{4,12},{8,16},{12,20},{16,24},{20,28},{24,0},{28,4},{1,9},{5... | collective-permute-start | bytes 442376 | tf_op jit(solution)/shard_map/ppermute | solution.py:780
  138.1 12.5 %collective-permute-start.31 = (bf16[96,768]{1,0:T(8,128)(2,1)S(1)}, bf16[96,768]{1,0:T(8,128)(2,1)S(1)}, u32[]{:S(2)}, u32[]{:S(2)}) collective-permute-start(bf16[96,768]{1,0:T(8,128)(2,1)S(1)} %get-tuple-element.125), channel_id=1, source_target_pairs={{0,16},{4,20},{8,24},{12,28},{16,0},{20,4},{24,8},{28,12},{1,17},{... | collective-permute-start | bytes 442376 | tf_op jit(solution)/shard_map/ppermute | solution.py:780
  140.8 9.9 %collective-permute-start.32 = (bf16[96,768]{1,0:T(8,128)(2,1)S(1)}, bf16[96,768]{1,0:T(8,128)(2,1)S(1)}, u32[]{:S(2)}, u32[]{:S(2)}) collective-permute-start(bf16[96,768]{1,0:T(8,128)(2,1)S(1)} %get-tuple-element.126), channel_id=1, source_target_pairs={{0,24},{4,28},{8,0},{12,4},{16,8},{20,12},{24,16},{28,20},{1,25},{... | collective-permute-start | bytes 442376 | tf_op jit(solution)/shard_map/ppermute | solution.py:780
  145.0 12.2 %collective-permute-start.7 = (bf16[2,256,768]{2,1,0:T(8,128)(2,1)}, bf16[2,256,768]{2,1,0:T(8,128)(2,1)S(1)}, u32[]{:S(2)}, u32[]{:S(2)}) collective-permute-start(bf16[2,256,768]{2,1,0:T(8,128)(2,1)} %copy-done.22), channel_id=1, source_target_pairs={{0,1},{1,0},{2,3},{3,2},{4,5},{5,4},{6,7},{7,6},{8,9},{9,8},{10,11... | collective-permute-start | bytes 2359304 | tf_op jit(solution)/shard_map/ppermute | solution.py:765
  153.8 16.3 %collective-permute-start.21 = (bf16[2,4,96,384]{3,2,1,0:T(8,128)(2,1)S(1)}, bf16[2,4,96,384]{3,2,1,0:T(8,128)(2,1)S(1)}, u32[]{:S(2)}, u32[]{:S(2)}) collective-permute-start(bf16[2,4,96,384]{3,2,1,0:T(8,128)(2,1)S(1)} %dynamic-slice_bitcast_fusion.2), channel_id=1, source_target_pairs={{0,4},{4,0},{8,12},{12,8},{16,20},{20,16},{24,28},{28,24},{1,5},{5... | collective-permute-start | bytes 1769480 | tf_op jit(solution)/shard_map/ppermute | solution.py:775
  155.6 16.3 %collective-permute-start.19 = (bf16[4,2,96,384]{3,2,0,1:T(8,128)(2,1)S(1)}, bf16[4,2,96,384]{3,2,0,1:T(8,128)(2,1)S(1)}, u32[]{:S(2)}, u32[]{:S(2)}) collective-permute-start(bf16[4,2,96,384]{3,2,0,1:T(8,128)(2,1)S(1)} %bitcast.193), channel_id=1, source_target_pairs={{0,2},{1,3},{2,0},{3,1},{4,6},{5,7},{6,4},{7,5},{8,10},{9,11},{10,... | collective-permute-start | bytes 1769480 | tf_op jit(solution)/shard_map/ppermute | solution.py:770
  157.4 22.9 %collective-permute-start.8 = (bf16[256,768]{1,0:T(8,128)(2,1)S(1)}, bf16[256,768]{1,0:T(8,128)(2,1)S(1)}, u32[]{:S(2)}, u32[]{:S(2)}) collective-permute-start(bf16[256,768]{1,0:T(8,128)(2,1)S(1)} %fusion.14), channel_id=1, source_target_pairs={{0,2},{1,3},{2,0},{3,1},{4,6},{5,7},{6,4},{7,5},{8,10},{9,11},{10,... | collective-permute-start | bytes 1179656 | tf_op jit(solution)/shard_map/ppermute | solution.py:770
  161.2 27.9 %collective-permute-start.13 = (bf16[2,4,104,384]{3,2,1,0:T(8,128)(2,1)S(1)}, bf16[2,4,104,384]{3,2,1,0:T(8,128)(2,1)S(1)}, u32[]{:S(2)}, u32[]{:S(2)}) collective-permute-start(bf16[2,4,104,384]{3,2,1,0:T(8,128)(2,1)S(1)} %dynamic-slice_bitcast_fusion), channel_id=1, source_target_pairs={{0,4},{4,0},{8,12},{12,8},{16,20},{20,16},{24,28},{28,24},{1,5},{5... | collective-permute-start | bytes 1916936 | tf_op jit(solution)/shard_map/ppermute | solution.py:775
  170.3 16.4 %collective-permute-start.22 = (bf16[4,96,384]{2,1,0:T(8,128)(2,1)S(1)}, bf16[4,96,384]{2,1,0:T(8,128)(2,1)S(1)}, u32[]{:S(2)}, u32[]{:S(2)}) collective-permute-start(bf16[4,96,384]{2,1,0:T(8,128)(2,1)S(1)} %dynamic-slice_bitcast_fusion.7), channel_id=1, source_target_pairs={{0,2},{1,3},{2,0},{3,1},{4,6},{5,7},{6,4},{7,5},{8,10},{9,11},{10,... | collective-permute-start | bytes 884744 | tf_op jit(solution)/shard_map/ppermute | solution.py:770
  172.1 16.9 %collective-permute-start.20 = (bf16[4,96,384]{2,1,0:T(8,128)(2,1)S(1)}, bf16[4,96,384]{2,1,0:T(8,128)(2,1)S(1)}, u32[]{:S(2)}, u32[]{:S(2)}) collective-permute-start(bf16[4,96,384]{2,1,0:T(8,128)(2,1)S(1)} %dynamic-slice_bitcast_fusion.8), channel_id=1, source_target_pairs={{0,4},{4,0},{8,12},{12,8},{16,20},{20,16},{24,28},{28,24},{1,5},{5... | collective-permute-start | bytes 884744 | tf_op jit(solution)/shard_map/ppermute | solution.py:775
  173.8 6.6 %copy-start.11 = (f32[256,768]{1,0:T(8,128)S(1)}, f32[256,768]{1,0:T(8,128)}, u32[]{:S(2)}) copy-start(f32[256,768]{1,0:T(8,128)} %copy-done.10) | copy-start | bytes 2359300
  173.8 26.5 %collective-permute-start.10 = (bf16[4,2,104,384]{3,2,0,1:T(8,128)(2,1)S(1)}, bf16[4,2,104,384]{3,2,0,1:T(8,128)(2,1)S(1)}, u32[]{:S(2)}, u32[]{:S(2)}) collective-permute-start(bf16[4,2,104,384]{3,2,0,1:T(8,128)(2,1)S(1)} %bitcast.192), channel_id=1, source_target_pairs={{0,2},{1,3},{2,0},{3,1},{4,6},{5,7},{6,4},{7,5},{8,10},{9,11},{10,... | collective-permute-start | bytes 1916936 | tf_op jit(solution)/shard_map/ppermute | solution.py:770
  189.4 17.9 %collective-permute-start.14 = (bf16[4,104,384]{2,1,0:T(8,128)(2,1)S(1)}, bf16[4,104,384]{2,1,0:T(8,128)(2,1)S(1)}, u32[]{:S(2)}, u32[]{:S(2)}) collective-permute-start(bf16[4,104,384]{2,1,0:T(8,128)(2,1)S(1)} %dynamic-slice_bitcast_fusion.3), channel_id=1, source_target_pairs={{0,2},{1,3},{2,0},{3,1},{4,6},{5,7},{6,4},{7,5},{8,10},{9,11},{10,... | collective-permute-start | bytes 958472 | tf_op jit(solution)/shard_map/ppermute | solution.py:770
  200.6 7.1 %collective-permute-start.11 = (bf16[4,104,384]{2,1,0:T(8,128)(2,1)S(1)}, bf16[4,104,384]{2,1,0:T(8,128)(2,1)S(1)}, u32[]{:S(2)}, u32[]{:S(2)}) collective-permute-start(bf16[4,104,384]{2,1,0:T(8,128)(2,1)S(1)} %dynamic-slice_bitcast_fusion.4), channel_id=1, source_target_pairs={{0,4},{4,0},{8,12},{12,8},{16,20},{20,16},{24,28},{28,24},{1,5},{5... | collective-permute-start | bytes 958472 | tf_op jit(solution)/shard_map/ppermute | solution.py:775
  201.2 11.9 %collective-permute-start.23 = (bf16[192,384]{1,0:T(8,128)(2,1)S(1)}, bf16[192,384]{1,0:T(8,128)(2,1)S(1)}, u32[]{:S(2)}, u32[]{:S(2)}) collective-permute-start(bf16[192,384]{1,0:T(8,128)(2,1)S(1)} %get-tuple-element.127), channel_id=1, source_target_pairs={{0,8},{4,12},{8,16},{12,20},{16,24},{20,28},{24,0},{28,4},{1,9},{5... | collective-permute-start | bytes 442376 | tf_op jit(solution)/shard_map/ppermute | solution.py:780
  204.9 14.8 %collective-permute-start.24 = (bf16[192,384]{1,0:T(8,128)(2,1)S(1)}, bf16[192,384]{1,0:T(8,128)(2,1)S(1)}, u32[]{:S(2)}, u32[]{:S(2)}) collective-permute-start(bf16[192,384]{1,0:T(8,128)(2,1)S(1)} %get-tuple-element.128), channel_id=1, source_target_pairs={{0,16},{4,20},{8,24},{12,28},{16,0},{20,4},{24,8},{28,12},{1,17},{... | collective-permute-start | bytes 442376 | tf_op jit(solution)/shard_map/ppermute | solution.py:780
  206.5 13.2 %collective-permute-start.25 = (bf16[192,384]{1,0:T(8,128)(2,1)S(1)}, bf16[192,384]{1,0:T(8,128)(2,1)S(1)}, u32[]{:S(2)}, u32[]{:S(2)}) collective-permute-start(bf16[192,384]{1,0:T(8,128)(2,1)S(1)} %get-tuple-element.129), channel_id=1, source_target_pairs={{0,24},{4,28},{8,0},{12,4},{16,8},{20,12},{24,16},{28,20},{1,25},{... | collective-permute-start | bytes 442376 | tf_op jit(solution)/shard_map/ppermute | solution.py:780
  207.8 12.7 %collective-permute-start.15 = (bf16[208,384]{1,0:T(8,128)(2,1)S(1)}, bf16[208,384]{1,0:T(8,128)(2,1)S(1)}, u32[]{:S(2)}, u32[]{:S(2)}) collective-permute-start(bf16[208,384]{1,0:T(8,128)(2,1)S(1)} %get-tuple-element.121), channel_id=1, source_target_pairs={{0,8},{4,12},{8,16},{12,20},{16,24},{20,28},{24,0},{28,4},{1,9},{5... | collective-permute-start | bytes 479240 | tf_op jit(solution)/shard_map/ppermute | solution.py:780
  211.5 16.7 %collective-permute-start.16 = (bf16[208,384]{1,0:T(8,128)(2,1)S(1)}, bf16[208,384]{1,0:T(8,128)(2,1)S(1)}, u32[]{:S(2)}, u32[]{:S(2)}) collective-permute-start(bf16[208,384]{1,0:T(8,128)(2,1)S(1)} %get-tuple-element.122), channel_id=1, source_target_pairs={{0,16},{4,20},{8,24},{12,28},{16,0},{20,4},{24,8},{28,12},{1,17},{... | collective-permute-start | bytes 479240 | tf_op jit(solution)/shard_map/ppermute | solution.py:780
  213.1 15.1 %collective-permute-start.17 = (bf16[208,384]{1,0:T(8,128)(2,1)S(1)}, bf16[208,384]{1,0:T(8,128)(2,1)S(1)}, u32[]{:S(2)}, u32[]{:S(2)}) collective-permute-start(bf16[208,384]{1,0:T(8,128)(2,1)S(1)} %get-tuple-element.123), channel_id=1, source_target_pairs={{0,24},{4,28},{8,0},{12,4},{16,8},{20,12},{24,16},{28,20},{1,25},{... | collective-permute-start | bytes 479240 | tf_op jit(solution)/shard_map/ppermute | solution.py:780
  (35 other events, 68.2 us)
